TPU v7x, 256 devices: a whole 4x4x8 slice. The times are simulated.
256 devices in a mesh: px: 32 (over y, z_lo, core), py: 8 (over x, z_hi).
Axes of the slice: x: 4, y: 4, z: 8 (z_hi: 2, z_lo: 4; z = z_hi * 4 + z_lo), core: 2. Of those that a mesh axis runs over, the one named last changes fastest.
Arguments:
- features: bfloat16 [32, 128, 256, 256], P(None, 'py', 'px'), may hold values from -6 to 6
- cotangent: bfloat16 [32, 128, 256, 256], P(None, 'py', 'px'), may hold values from -6 to 6
- pointwise_fine: bfloat16 [32, 32], replicated, may hold values from -1 to 1
- spectral_fine: float32 [2, 32, 32, 16, 32, 32], P(None, None, None, None, 'px', 'py'), may hold values from -16 to 16
- lift_weight: bfloat16 [32, 64], replicated, may hold values from -8 to 8
- pointwise_coarse: bfloat16 [64, 64], replicated, may hold values from -0.75 to 0.75
- spectral_coarse: float32 [2, 64, 64, 16, 32, 32], P(None, None, None, None, 'px', 'py'), may hold values from -1.5 to 1.5
- project_weight: bfloat16 [64, 32], replicated, may hold values from -0.75 to 0.75
Outputs:
- layer_out: bfloat16 [32, 128, 256, 256], P(None, 'py', 'px')
- grad_features: bfloat16 [32, 128, 256, 256], P(None, 'py', 'px')
- grad_spectral: float32 [2, 32, 32, 16, 32, 32], P(None, None, None, None, 'px', 'py')
All inputs are finite; a program needn't handle non-finite values.
Results may differ from a plain program's by a relative error of at most 0.001.
Values sent between devices are 32-bit elements; how exact they have to be, the bound alone decides.
A program may use at most 128 MiB of HBM per device.

v0:
```python
import functools
import math

import jax
import jax.numpy as jnp
import numpy as np
from jax import lax
from jax.experimental import pallas as pl
from jax.experimental.pallas import tpu as pltpu
from jax.sharding import PartitionSpec as P

M = 16
F32 = jnp.float32
BF16 = jnp.bfloat16
MESH = pl.DeviceIdType.MESH
NPX, NPY = 32, 8
PAIRS = 320
ROOT = math.sqrt(2.0 / math.pi)


def single(table):
    return np.asarray(table, np.float64).astype(np.float32)


def signed(index):
    return np.where(index < M, index, index - 2 * M)


def turn(freq, cell, count):
    return (np.asarray(freq) * np.asarray(cell) % count) * (2.0 * np.pi / count)


@functools.cache
def tables():
    out = {}
    x = np.arange(256)
    rows = np.zeros((40, 256))
    for j in range(17):
        angle = turn(j, x, 256)
        if j == 0:
            rows[0] = rows[1] = 1.0
        else:
            rows[2 * j] = np.cos(angle)
            rows[2 * j + 1] = -np.sin(angle) if j < 16 else np.sin(angle)
    out["tx"] = single(rows)
    inv = rows.copy()
    inv[1] = 0.0
    out["ix"] = single(inv)

    ky = np.arange(32)
    theta = turn(signed(ky)[:, None], np.arange(256)[None, :], 256)
    cos, sin = np.cos(theta), np.sin(theta)
    zero = np.zeros_like(cos)
    plus = (((cos, sin), (-sin, cos)))
    minus = (((cos, -sin), (-sin, -cos)))
    from0 = (((cos, zero), (-sin, zero)))
    from1 = (((zero, cos), (zero, -sin)))
    none = (((zero, zero), (zero, zero)))
    kinds = [(plus, minus), (minus, plus), (from0, from1), (plus, none), (none, plus)]
    ty = np.zeros((5, 2, 2, 8, 2, 4, 32, 2, 8))
    for k, pair in enumerate(kinds):
        for q in range(2):
            for r1 in range(2):
                for r in range(2):
                    block = pair[q][r1][r].reshape(8, 4, 32, 8)
                    for dup in range(2):
                        ty[k, r1, q, :, dup, :, :, r, :] = block
    ty = ty.reshape(5, 256, 512)
    out["ty"] = single(ty)

    ti = np.zeros((5, 32, 2, 8, 2, 2, 8, 2, 4))

    def add(k, rout, q, part, sign):
        c = cos.T.reshape(32, 8, 8, 4)
        s = sin.T.reshape(32, 8, 8, 4)
        if part == 0:
            coef = {(0, 0): c, (1, 1): -c, (0, 1): -s, (1, 0): -s}
        else:
            coef = {(0, 0): s, (1, 1): -s, (0, 1): c, (1, 0): c}
        for (cs, r), value in coef.items():
            ti[k, :, rout, :, cs, q, :, r, :] += sign * value

    for k, first in ((0, 1.0), (1, -1.0)):
        add(k, 0, 0, 0, 1.0)
        add(k, 0, 1, 0, 1.0)
        add(k, 1, 0, 1, first)
        add(k, 1, 1, 1, -first)
    add(2, 0, 0, 0, 1.0)
    add(2, 1, 1, 0, 1.0)
    for k, q in ((3, 0), (4, 1)):
        add(k, 0, q, 0, 1.0)
        add(k, 1, q, 1, 1.0)
    out["ti"] = single(ti.reshape(5, 512, 256))

    kz = np.arange(16)
    zf = np.zeros((8, 2, 8, 16, 2, 8, 16))
    zi = np.zeros((8, 8, 16, 2, 8, 16))
    for b in range(8):
        phi = turn(kz[None, :], (b * 16 + np.arange(16))[:, None], 128)
        for c in range(8):
            zf[b, 0, c, :, 0, c, :] = np.cos(phi)
            zf[b, 1, c, :, 0, c, :] = np.sin(phi)
            zf[b, 0, c, :, 1, c, :] = -np.sin(phi)
            zf[b, 1, c, :, 1, c, :] = np.cos(phi)
            zi[b, c, :, 0, c, :] = np.cos(phi).T
            zi[b, c, :, 1, c, :] = np.sin(phi).T
    out["zf"] = single(zf.reshape(8, 256, 256))
    out["zi"] = single(zi.reshape(8, 128, 256))

    kx = np.arange(32)
    alpha = turn(signed(kx)[:, None], (x // 4)[None, :], 64)
    txc = np.stack([np.cos(alpha), -np.sin(alpha)], axis=1).reshape(64, 256)
    out["txc"] = single(txc)
    theta = turn(signed(ky)[:, None], np.arange(64)[None, :], 64)
    cos, sin = np.cos(theta), np.sin(theta)
    tyc = np.zeros((2, 8, 2, 4, 32, 2, 4))
    plus = ((cos, sin), (-sin, cos))
    for r1 in range(2):
        for r in range(2):
            for dup in range(2):
                tyc[r1, :, dup, :, :, r, :2] = plus[r1][r].reshape(8, 4, 32, 2)
    out["tyc"] = single(tyc.reshape(128, 256))
    tic = np.zeros((32, 2, 2, 2, 8, 2, 4))
    c = cos.T.reshape(32, 2, 8, 4)
    s = sin.T.reshape(32, 2, 8, 4)
    for (rout, cs, r), value in {
        (0, 0, 0): c, (0, 1, 1): -c, (0, 0, 1): -s, (0, 1, 0): -s,
        (1, 0, 0): s, (1, 1, 1): -s, (1, 0, 1): c, (1, 1, 0): c,
    }.items():
        tic[:, rout, :, cs, :, r, :] = value
    out["tic"] = single(tic.reshape(128, 128))
    zfc = np.zeros((8, 2, 2, 4, 2, 32, 16))
    zic = np.zeros((8, 16, 2, 64, 4))
    for b in range(8):
        phi = turn(kz[None, :], (b * 4 + np.arange(4))[:, None], 32)
        zfc[b, 0, :, :, 0] = np.cos(phi)[None, :, None, :]
        zfc[b, 1, :, :, 0] = np.sin(phi)[None, :, None, :]
        zfc[b, 0, :, :, 1] = -np.sin(phi)[None, :, None, :]
        zfc[b, 1, :, :, 1] = np.cos(phi)[None, :, None, :]
        zic[b, :, 0] = np.cos(phi).T[:, None, :]
        zic[b, :, 1] = np.sin(phi).T[:, None, :]
    out["zfc"] = single(zfc.reshape(8, 2, 8, 1024))
    out["zic"] = single(zic.reshape(8, 16, 512))
    alpha = turn(signed(kx)[:, None], np.arange(64)[None, :], 64)
    ixc = np.zeros((32, 2, 2, 2, 64))
    for big in range(2):
        ixc[:, 0, big, big] = np.cos(alpha)
        ixc[:, 1, big, big] = -np.sin(alpha)
    out["ixc"] = single(ixc.reshape(128, 128))
    return out


def split(value):
    high = value.astype(BF16)
    return high, (value - high.astype(F32)).astype(BF16)


def dot(left, right, dims=((1,), (0,))):
    return lax.dot_general(left, right, (dims, ((), ())), preferred_element_type=F32)


def dot3(left_high, left_low, right_high, right_low, dims=((1,), (0,))):
    return (
        dot(left_high, right_high, dims)
        + dot(left_high, right_low, dims)
        + dot(left_low, right_high, dims)
    )


def iota(shape, dim):
    return lax.broadcasted_iota(jnp.int32, shape, dim)


def ones_where(condition):
    return jnp.where(condition, 1.0, 0.0).astype(BF16)


def kron_eye(first, shift):
    rows, m = first.shape
    spread = ones_where(iota((m, m << shift), 0) == (iota((m, m << shift), 1) >> shift))
    full = dot(first.astype(BF16), spread)
    low = (1 << shift) - 1
    shape = (rows, m << shift)
    return jnp.where((iota(shape, 0) & low) == (iota(shape, 1) & low), full, 0.0).astype(BF16)


def rows_of(weight, n, shift, axis):
    pick = ones_where((iota((n << shift, n), 0) >> shift) == iota((n << shift, n), 1))
    return dot(pick, weight, ((1,), (axis,)))


def to_modes(packed, count):
    lanes = count * 16
    real = jnp.concatenate([packed[0:4]] * 16, axis=0)
    imag = jnp.concatenate([packed[4:8]] * 16, axis=0)
    mask = (iota((64, lanes), 0) >> 2) == (iota((64, lanes), 1) & 15)
    wide = jnp.concatenate([jnp.where(mask, real, 0.0), jnp.where(mask, imag, 0.0)], axis=0)
    pick = ones_where((iota((lanes, count), 0) >> 4) == iota((lanes, count), 1))
    high, low = split(wide)
    modes = dot(high, pick) + dot(low, pick)
    return modes[:64], modes[64:]


def from_modes(real, imag, count):
    lanes = count * 16
    high, low = split(jnp.concatenate([real, imag], axis=0))
    spread = ones_where(iota((count, lanes), 0) == (iota((count, lanes), 1) >> 4))
    wide = dot(high, spread) + dot(low, spread)
    mask = ((iota((128, lanes), 0) & 63) >> 2) == (iota((128, lanes), 1) & 15)
    high, low = split(jnp.where(mask, wide, 0.0))
    shape = (8, 128)
    total = ones_where(
        ((iota(shape, 1) >> 6) == (iota(shape, 0) >> 2)) & ((iota(shape, 1) & 3) == (iota(shape, 0) & 3))
    )
    return dot(total, high) + dot(total, low)


def column(values, index):
    return values[:, index : index + 1]


def mix_modes(weight_ref, real, imag, count):
    out_real = jnp.zeros((64, count), F32)
    out_imag = jnp.zeros((64, count), F32)
    for i in range(count):
        w0, w1 = weight_ref[0, i], weight_ref[1, i]
        a, b = column(real, i), column(imag, i)
        out_real = out_real + (w0 * a - w1 * b)
        out_imag = out_imag + (w0 * b + w1 * a)
    return out_real, out_imag


def mode_factor(cells):
    return jnp.where(iota((64, 1), 0) < 4, 1.0 / cells, 2.0 / cells).astype(F32)


def tanh_gelu(value):
    return 0.5 * value * (1.0 + jnp.tanh(ROOT * (value + 0.044715 * value * value * value)))


def kernel(
    feat, cot_hbm, w_fine, spec_hbm, lift, w_coarse, spec_c_hbm, project,
    tx_in, ix_in, ty_hbm, zf_hbm, zi_hbm, ti_hbm, txc_in, tyc_in, zfc_hbm, zic_hbm, tic_in, ixc_in,
    layer_out, grad_out, gspec,
    b0, b1, b2, fy, gph, gpl, cot, spec, spec_c,
    ty, tye, zf, zi, ti, tie, zfc, zic, zfull_h, zfull_l, zifull_h, zifull_l,
    tx, ix, ty_s, tye_s, zf_s, zi_s, ti_s, tie_s,
    wk, wkt, yc, rst, rst2, modes,
    s_buf, rx, rxe, ex, re_buf, hq, ri, sv, sve, g_buf,
    sc, rc, exc, rec, hc, ric, svc, gc,
    load_sem, px_send, px_recv, pxe_send, pxe_recv, py_send, py_recv, pye_send,
    c_send, c_recv,
):
    me = lax.axis_index("px")
    mine = lax.axis_index("py")
    partner = lax.rem(NPX - me, NPX)
    upper = lax.div(me + 15, 32)
    is0 = 1 - lax.div(me + 31, 32)
    is16 = lax.div(me, 16) * (1 - upper)
    kind = upper + 2 * is0 + 3 * is16
    regular = 1 - is0 - is16

    loads = [
        (cot_hbm, cot), (spec_hbm, spec), (spec_c_hbm, spec_c),
        (ty_hbm.at[kind], ty), (ty_hbm.at[4], tye), (zf_hbm.at[mine], zf), (zi_hbm.at[mine], zi),
        (ti_hbm.at[kind], ti), (ti_hbm.at[4], tie), (zfc_hbm.at[mine], zfc), (zic_hbm.at[mine], zic),
    ]
    loads = [pltpu.make_async_copy(a, b, load_sem.at[n]) for n, (a, b) in enumerate(loads)]
    for load in loads:
        load.start()

    barrier = pltpu.get_barrier_semaphore()

    def greet(t, carry):
        pl.semaphore_signal(
            barrier, inc=1, device_id={"px": lax.rem(me + t, NPX), "py": mine}, device_id_type=MESH
        )
        return carry

    lax.fori_loop(1, NPX, greet, 0)

    def greet_own(t, carry):
        pl.semaphore_signal(
            barrier, inc=1, device_id={"px": me, "py": lax.rem(mine + t, NPY)}, device_id_type=MESH
        )
        return carry

    lax.fori_loop(1, NPY, greet_own, 0)

    @pl.when(regular == 1)
    def _():
        def greet_partner(t, carry):
            pl.semaphore_signal(
                barrier, inc=1, device_id={"px": partner, "py": lax.rem(mine + t, NPY)},
                device_id_type=MESH,
            )
            return carry

        lax.fori_loop(1, NPY, greet_partner, 0)

    def pair_row(d):
        h = lax.div(d + 15, 32)
        return h, pl.multiple_of(16 * (d * (1 - 2 * h) + 32 * h), 16)

    def px_forward(n):
        def send(t, carry):
            d = lax.rem(me + t, NPX)
            h, row = pair_row(d)
            pltpu.make_async_remote_copy(
                s_buf.at[n, h, :, pl.ds(row, 16)], rx.at[n, :, pl.ds(pl.multiple_of(16 * me, 16), 16)],
                px_send.at[2 * n], px_recv.at[2 * n], device_id={"px": d, "py": mine}, device_id_type=MESH,
            ).start()
            return carry

        lax.fori_loop(1, NPX, send, 0)
        h, row = pair_row(me)
        pltpu.make_async_copy(
            s_buf.at[n, h, :, pl.ds(row, 16)], rx.at[n, :, pl.ds(pl.multiple_of(16 * me, 16), 16)], px_recv.at[2 * n]
        ).start()

        @pl.when(is16 == 0)
        def _():
            pltpu.make_async_remote_copy(
                s_buf.at[n, 1, :, pl.ds(256, 16)], rxe.at[n, :, pl.ds(pl.multiple_of(16 * me, 16), 16)],
                pxe_send.at[2 * n], pxe_recv.at[2 * n], device_id={"px": 16, "py": mine}, device_id_type=MESH,
            ).start()

        @pl.when(is16 == 1)
        def _():
            pltpu.make_async_copy(
                s_buf.at[n, 1, :, pl.ds(256, 16)], rxe.at[n, :, pl.ds(pl.multiple_of(16 * me, 16), 16)],
                pxe_recv.at[2 * n],
            ).start()

    def px_forward_wait(n):
        pltpu.make_async_copy(rx.at[n], rx.at[n], px_recv.at[2 * n]).wait()

        @pl.when(is16 == 1)
        def _():
            pltpu.make_async_copy(rxe.at[n], rxe.at[n], pxe_recv.at[2 * n]).wait()

    def px_inverse(n):
        h, row = pair_row(me)

        def send(t, carry):
            d = lax.rem(me + t, NPX)
            pltpu.make_async_remote_copy(
                sv.at[n, :, pl.ds(pl.multiple_of(16 * d, 16), 16)], g_buf.at[n, h, :, pl.ds(row, 16)],
                px_send.at[2 * n + 1], px_recv.at[2 * n + 1],
                device_id={"px": d, "py": mine}, device_id_type=MESH,
            ).start()
            return carry

        lax.fori_loop(1, NPX, send, 0)
        pltpu.make_async_copy(
            sv.at[n, :, pl.ds(pl.multiple_of(16 * me, 16), 16)], g_buf.at[n, h, :, pl.ds(row, 16)],
            px_recv.at[2 * n + 1],
        ).start()

        @pl.when(is16 == 1)
        def _():
            def send_extra(t, carry):
                d = lax.rem(me + t, NPX)
                pltpu.make_async_remote_copy(
                    sve.at[n, :, pl.ds(pl.multiple_of(16 * d, 16), 16)], g_buf.at[n, 1, :, pl.ds(256, 16)],
                    pxe_send.at[2 * n + 1], pxe_recv.at[2 * n + 1],
                    device_id={"px": d, "py": mine}, device_id_type=MESH,
                ).start()
                return carry

            lax.fori_loop(1, NPX, send_extra, 0)
            pltpu.make_async_copy(
                sve.at[n, :, pl.ds(pl.multiple_of(16 * me, 16), 16)], g_buf.at[n, 1, :, pl.ds(256, 16)],
                pxe_recv.at[2 * n + 1],
            ).start()

    def px_inverse_wait(n):
        pltpu.make_async_copy(rx.at[n], rx.at[n], px_recv.at[2 * n + 1]).wait()
        some = g_buf.at[n, 1, :, pl.ds(256, 16)]
        pltpu.make_async_copy(some, some, pxe_recv.at[2 * n + 1]).wait()

    def py_exchange(slot, source, target):
        def send(t, carry):
            p = lax.rem(mine + t, NPY)
            for q, to in ((0, me), (1, partner)):
                pltpu.make_async_remote_copy(
                    source(q, p), target.at[8 * q + mine], py_send.at[slot], py_recv.at[slot],
                    device_id={"px": to, "py": p}, device_id_type=MESH,
                ).start()
            return carry

        lax.fori_loop(1, NPY, send, 0)
        pltpu.make_async_copy(source(0, mine), target.at[mine], py_recv.at[slot]).start()

        @pl.when(regular == 1)
        def _():
            pltpu.make_async_remote_copy(
                source(1, mine), target.at[8 + mine], pye_send.at[slot], py_recv.at[slot],
                device_id={"px": partner, "py": mine}, device_id_type=MESH,
            ).start()

        @pl.when(regular == 0)
        def _():
            pltpu.make_async_copy(source(1, mine), target.at[8 + mine], py_recv.at[slot]).start()

    def py_wait(slot, target):
        pltpu.make_async_copy(target, target, py_recv.at[slot]).wait()

    def coarse_px(slot, source, target):
        there = target.at[pl.ds(pl.multiple_of(8 * me, 8), 8)]

        def send(t, carry):
            d = lax.rem(me + t, NPX)
            pltpu.make_async_remote_copy(
                source.at[pl.ds(pl.multiple_of(8 * d, 8), 8)], there, c_send.at[slot], c_recv.at[slot],
                device_id={"px": d, "py": mine}, device_id_type=MESH,
            ).start()
            return carry

        lax.fori_loop(1, NPX, send, 0)
        pltpu.make_async_copy(source.at[pl.ds(pl.multiple_of(8 * me, 8), 8)], there, c_recv.at[slot]).start()

    def coarse_py(slot, source, target):
        def send(t, carry):
            p = lax.rem(mine + t, NPY)
            pltpu.make_async_remote_copy(
                source(p), target.at[mine], c_send.at[slot], c_recv.at[slot],
                device_id={"px": me, "py": p}, device_id_type=MESH,
            ).start()
            return carry

        lax.fori_loop(1, NPY, send, 0)
        pltpu.make_async_copy(source(mine), target.at[mine], c_recv.at[slot]).start()

    def coarse_wait(slot, target):
        pltpu.make_async_copy(target, target, c_recv.at[slot]).wait()

    def tiles(ref, n):
        return jnp.concatenate([ref[n, 0], ref[n, 1]], axis=1)

    def put_tiles(ref, n, value):
        ref[n, 0] = value[:, :128]
        ref[n, 1] = value[:, 128:]

    def store_pairs(n, y, both):
        for h in range(2):
            for t in range(2):
                at = 256 * h + 128 * t
                s_buf[n, h, t, pl.ds(y, 40, stride=8), :] = both[:, at : at + 128]

    def fix_zero(n):
        s_buf[n, 0, :, pl.ds(8, 8), :] = s_buf[n, 1, :, pl.ds(0, 8), :]

    def forward_yz(n):
        high, low = split(tiles(rx, n))
        yc[...] = dot3(ty_s[0], ty_s[1], high, low)

        @pl.when(is16 == 1)
        def _():
            high, low = split(tiles(rxe, n))
            yc[...] += dot3(tye_s[0], tye_s[1], high, low)

        dup = ((iota((128, 128), 0) >> 2) & 1) == 0
        for t in range(2):
            lanes = pl.ds(128 * t, 128)
            both = jnp.concatenate([yc[pl.ds(0, 128), lanes], yc[pl.ds(128, 128), lanes]], axis=1)
            high, low = split(both)
            full = dot3(high, low, zf_s[0], zf_s[1])
            picked = jnp.where(dup, full[:, :128], full[:, 128:])
            ex[n, :, :, lanes] = picked.reshape(16, 8, 128)

    def gather_modes(n):
        slot0 = jnp.sum(re_buf[n, 0:8], axis=0)
        slot1 = jnp.sum(re_buf[n, 8:16], axis=0)
        swap = upper == 1
        first = jnp.where(swap, slot1, slot0)
        second = jnp.where(swap, slot0, slot1)
        return to_modes(jnp.concatenate([first, second], axis=1), 32)

    def spread_modes(n, real, imag):
        packed = from_modes(real, imag, 32)
        first, second = packed[:, :256], packed[:, 256:]
        swap = upper == 1
        hq[n, 0] = jnp.where(swap, second, first)
        hq[n, 1] = jnp.where(swap, first, second)

    def inverse_zy(n):
        value = ri[n].reshape(128, 256)
        parts = []
        for t in range(2):
            high, low = split(value[:, 128 * t : 128 * t + 128])
            parts.append(dot3(high, low, zi_s[0], zi_s[1]))
        stacked = jnp.concatenate(
            [
                jnp.concatenate([parts[0][:, :128], parts[1][:, :128]], axis=1),
                jnp.concatenate([parts[0][:, 128:], parts[1][:, 128:]], axis=1),
            ],
            axis=0,
        )
        high, low = split(stacked)
        put_tiles(sv, n, dot3(ti_s[0], ti_s[1], high, low))

        @pl.when(is16 == 1)
        def _():
            put_tiles(sve, n, dot3(tie_s[0], tie_s[1], high, low))

    def inverse_x(n, y):
        parts = [
            g_buf[n, h, t, pl.ds(y, 40, stride=8), :] for h in range(2) for t in range(2)
        ]
        value = jnp.concatenate(parts, axis=1)
        high = value.astype(BF16).astype(F32)
        stacked = jnp.concatenate([high, value - high, high, jnp.zeros((8, 512), F32)], axis=0)
        return dot(stacked.T.astype(BF16), ix[...])

    def fix_inverse_zero(n):
        g_buf[n, 1, :, pl.ds(0, 8), :] = g_buf[n, 0, :, pl.ds(8, 8), :]

    def take(ref, y):
        return jnp.concatenate(
            [ref[t, pl.ds(y, 512, stride=8), :] for t in range(2)], axis=1
        )

    def put(ref, y, value):
        for t in range(2):
            ref[t, pl.ds(y, 512, stride=8), :] = value[:, 128 * t : 128 * t + 128]

    def block(ref, y):
        rows = pl.ds(pl.multiple_of(512 * y, 512), 512)
        return jnp.concatenate([ref[0, rows, :], ref[1, rows, :]], axis=1)

    def put_block(ref, y, value):
        rows = pl.ds(pl.multiple_of(512 * y, 512), 512)
        ref[0, rows, :] = value[:, :128]
        ref[1, rows, :] = value[:, 128:]

    def unpack(ref, field):
        for t in range(2):
            ref[t] = field[:, :, pl.ds(128 * t, 128)].astype(F32).reshape(4096, 128)

    def pack(field, ref):
        for t in range(2):
            field[:, :, pl.ds(128 * t, 128)] = ref[t].reshape(512, 8, 128).astype(BF16)

    high, low = split(tx_in[...])
    tx[pl.ds(0, 40), :] = high
    tx[pl.ds(40, 40), :] = low
    high, low = split(ix_in[...])
    ix[...] = jnp.concatenate([high.astype(F32), high.astype(F32), low.astype(F32), jnp.zeros((8, 256), F32)], axis=0).astype(BF16)
    unpack(b0, feat)

    def analyse_x(y, carry):
        field = take(b0, y).astype(BF16)
        fy[y] = field
        both = dot(tx[...], field, ((1,), (1,)))
        store_pairs(0, y, both[:40] + both[40:])
        return carry

    lax.fori_loop(0, 8, analyse_x, 0)
    fix_zero(0)
    for n in range(2):
        g_buf[n, :, :, pl.ds(272, 48), :] = jnp.zeros((2, 2, 48, 128), F32)
        g_buf[n, 1, :, pl.ds(0, 16), :] = jnp.zeros((2, 16, 128), F32)
    sc[...] = jnp.zeros((256, 128), F32)

    pl.semaphore_wait(barrier, 38 + 7 * regular)
    px_forward(0)

    txc_high, txc_low = split(txc_in[...])
    pool = ones_where(iota((128, 512), 0) == (iota((128, 512), 1) >> 2))
    for big in range(2):
        total = dot(pool, fy[4 * big])
        for y in range(1, 4):
            total = total + dot(pool, fy[4 * big + y])
        total = total * (1.0 / 64.0)
        rst[big] = total
        high, low = split(total)
        part = dot3(txc_high, txc_low, high, low, ((1,), (1,)))
        sc[pl.ds(big, 64, stride=4), :] = part
    coarse_px(0, sc, rc)

    wk[...] = kron_eye(rows_of(w_fine[...], 32, 4, 1), 4)
    wkt[...] = kron_eye(rows_of(w_fine[...], 32, 4, 0), 4)

    def local(y, carry):
        put_block(b2, y, dot(wk[...], fy[y]))
        return carry

    lax.fori_loop(0, 8, local, 0)
    loads[0].wait()
    unpack(b1, cot)
    low_total = jnp.zeros((128, 128), F32)
    for big in range(2):
        gather = ones_where(iota((256, 128), 1) == 64 * big + (iota((256, 128), 0) >> 2))
        high, low = split(rst[big])
        low_total = low_total + dot(high, gather) + dot(low, gather)
    rst2[...] = low_total
    for n in range(1, 11):
        loads[n].wait()
    for whole, parts in ((ty, ty_s), (tye, tye_s), (zf, zf_s), (zi, zi_s), (ti, ti_s), (tie, tie_s)):
        high, low = split(whole[...])
        parts[0] = high
        parts[1] = low
    base_mask = (iota((128, 1024), 0) >> 2) == ((iota((128, 1024), 1) & 511) >> 4)
    for r in range(2):
        full = jnp.where(base_mask, jnp.concatenate([zfc[r]] * 16, axis=0), 0.0)
        high, low = split(full)
        zfull_h[pl.ds(128 * r, 128), :] = high
        zfull_l[pl.ds(128 * r, 128), :] = low

    def build(step, carry):
        rows = 128 * step + iota((128, 512), 0)
        keep = (rows >> 4) == ((iota((128, 512), 1) & 255) >> 2)
        high, low = split(jnp.where(keep, jnp.concatenate([zic[...]] * 8, axis=0), 0.0))
        at = pl.ds(pl.multiple_of(128 * step, 128), 128)
        zifull_h[at, :] = high
        zifull_l[at, :] = low
        return carry

    lax.fori_loop(0, 8, build, 0)

    px_forward_wait(0)
    forward_yz(0)
    py_exchange(0, lambda q, p: ex.at[0, 8 * q + p], re_buf.at[0])

    coarse_wait(0, rc)
    high, low = split(rc[...])
    along_y = dot3(*split(tyc_in[...]), high, low)
    high, low = split(jnp.concatenate([along_y[:64], along_y[64:]], axis=1))
    full = dot3(high, low, zfull_h[...], zfull_l[...])
    dup = ((iota((64, 512), 0) >> 2) & 1) == 0
    exc[...] = jnp.where(dup, full[:, :512], full[:, 512:]).reshape(8, 8, 512)
    coarse_py(1, lambda p: exc.at[p], rec)

    py_wait(0, re_buf.at[0])
    real, imag = gather_modes(0)
    modes[0] = real
    modes[1] = imag
    out_real, out_imag = mix_modes(spec, real, imag, 32)
    fine_factor = mode_factor(256.0 * 256.0 * 128.0)
    spread_modes(0, out_real * fine_factor, out_imag * fine_factor)
    py_exchange(1, lambda q, p: hq.at[0, q], ri.at[0])

    coarse_wait(1, rec)
    real, imag = to_modes(jnp.sum(rec[...], axis=0), 32)
    high, low = split(jnp.concatenate([real, imag], axis=0))
    lifted = dot(high, lift[...]) + dot(low, lift[...])
    out_real, out_imag = mix_modes(spec_c, lifted[:64], lifted[64:], 64)
    coarse_factor = mode_factor(64.0 * 64.0 * 32.0)
    hc[...] = from_modes(out_real * coarse_factor, out_imag * coarse_factor, 64)
    coarse_py(2, lambda p: hc, ric)

    py_wait(1, ri.at[0])
    inverse_zy(0)
    px_inverse(0)

    coarse_wait(2, ric)
    high, low = split(ric[...].reshape(64, 1024))
    along_z = dot3(high, low, zifull_h[...], zifull_l[...])
    high, low = split(jnp.concatenate([along_z[:, :256], along_z[:, 256:]], axis=0))
    along_y = dot3(*split(tic_in[...]), high, low)
    for hh in range(2):
        svc[pl.ds(hh, 128, stride=2), :] = along_y[:, 128 * hh : 128 * hh + 128]
    coarse_px(3, svc, gc)

    px_inverse_wait(0)
    fix_inverse_zero(0)

    def middle(y, carry):
        pre = block(b2, y) + inverse_x(0, y)
        square = pre * pre
        t = jnp.tanh(ROOT * pre * (1.0 + 0.044715 * square))
        half = 0.5 * (1.0 + t)
        put_block(b0, y, pre * half)
        slope = half + 0.5 * pre * (1.0 - t * t) * (ROOT + (3.0 * 0.044715 * ROOT) * square)
        grad = take(b1, y) * slope
        high, low = split(grad)
        gph[y] = high
        gpl[y] = low
        both = dot(tx[...], high, ((1,), (1,)))
        part = both[:40] + both[40:] + dot(tx[pl.ds(0, 40), :], low, ((1,), (1,)))
        store_pairs(1, y, part)
        return carry

    lax.fori_loop(0, 8, middle, 0)
    fix_zero(1)
    px_forward(1)

    def direct(y, carry):
        put_block(b1, y, dot(wkt[...], gph[y]) + dot(wkt[...], gpl[y]))
        return carry

    lax.fori_loop(0, 8, direct, 0)

    coarse_wait(3, gc)
    halves_out = []
    for hh in range(2):
        high, low = split(gc[pl.ds(hh, 128, stride=2), :].T)
        halves_out.append(dot3(high, low, *split(ixc_in[...])))
    spectral_part = jnp.concatenate(halves_out, axis=0)
    lift_wide = kron_eye(rows_of(lift[...], 64, 2, 1), 2)
    coarse_wide = kron_eye(rows_of(w_coarse[...], 64, 2, 1), 2)
    project_wide = kron_eye(rows_of(project[...], 32, 2, 0), 2)
    high, low = split(rst2[...])
    lifted = dot(lift_wide, high) + dot(lift_wide, low)
    high, low = split(lifted)
    coarse_pre = spectral_part + dot(coarse_wide, high) + dot(coarse_wide, low)
    high, low = split(tanh_gelu(coarse_pre))
    coarse_out = dot(project_wide, high) + dot(project_wide, low)
    out_high, out_low = split(coarse_out)
    widen = ones_where((iota((512, 128), 0) >> 2) == iota((512, 128), 1))
    for big in range(2):
        stretch = ones_where(iota((128, 256), 0) == 64 * big + (iota((128, 256), 1) >> 2))
        high, low = split(dot(out_high, stretch) + dot(out_low, stretch))
        prolonged = dot(widen, high) + dot(widen, low)
        for small in range(4):
            y = 4 * big + small
            put(b2, y, block(b0, y) + prolonged)
    pack(layer_out, b2)

    px_forward_wait(1)
    forward_yz(1)
    py_exchange(2, lambda q, p: ex.at[1, 8 * q + p], re_buf.at[1])
    py_wait(2, re_buf.at[1])
    real, imag = gather_modes(1)
    real, imag = real * fine_factor, imag * fine_factor
    lane = iota((64, 32), 1)
    pull_real = jnp.zeros((64, 32), F32)
    pull_imag = jnp.zeros((64, 32), F32)
    for i in range(32):
        w0, w1 = spec[0, i], spec[1, i]
        a = jnp.sum(w0 * real + w1 * imag, axis=1, keepdims=True)
        b = jnp.sum(w0 * imag - w1 * real, axis=1, keepdims=True)
        pull_real = jnp.where(lane == i, a, pull_real)
        pull_imag = jnp.where(lane == i, b, pull_imag)
    spread_modes(1, pull_real, pull_imag)
    py_exchange(3, lambda q, p: hq.at[1, q], ri.at[1])
    x_real, x_imag = modes[0], modes[1]
    for i in range(32):
        a, b = column(x_real, i), column(x_imag, i)
        gspec[0, i] = real * a + imag * b
        gspec[1, i] = imag * a - real * b
    py_wait(3, ri.at[1])
    inverse_zy(1)
    px_inverse(1)

    px_inverse_wait(1)
    fix_inverse_zero(1)

    def final(y, carry):
        put(b2, y, block(b1, y) + inverse_x(1, y))
        return carry

    lax.fori_loop(0, 8, final, 0)
    pack(grad_out, b2)

    for n in range(2):
        most = rx.at[n, :, pl.ds(0, 496)]
        for k in range(2):
            pltpu.make_async_copy(most, most, px_send.at[2 * n + k]).wait()

        @pl.when(is16 == 0)
        def _():
            some = rx.at[n, :, pl.ds(0, 16)]
            pltpu.make_async_copy(some, some, pxe_send.at[2 * n]).wait()

        @pl.when(is16 == 1)
        def _():
            pltpu.make_async_copy(most, most, pxe_send.at[2 * n + 1]).wait()

    for slot in range(4):
        most = ex.at[0, pl.ds(0, 14)]
        pltpu.make_async_copy(most, most, py_send.at[slot]).wait()

        @pl.when(regular == 1)
        def _():
            pltpu.make_async_copy(ex.at[0, 0], ex.at[0, 0], pye_send.at[slot]).wait()

    for slot, most in ((0, rc.at[pl.ds(0, 248)]), (1, exc.at[pl.ds(0, 7)]), (2, ric.at[pl.ds(0, 7)]), (3, gc.at[pl.ds(0, 248)])):
        pltpu.make_async_copy(most, most, c_send.at[slot]).wait()


def body(
    features, cotangent, pointwise_fine, spectral_fine, lift_weight, pointwise_coarse,
    spectral_coarse, project_weight,
):
    table = tables()
    fine = spectral_fine.transpose(0, 1, 3, 4, 5, 2).reshape(2, 32, 64, 32)
    coarse = spectral_coarse.transpose(0, 1, 3, 4, 5, 2).reshape(2, 64, 64, 64)
    vmem = pl.BlockSpec(memory_space=pltpu.VMEM)
    hbm = pl.BlockSpec(memory_space=pl.ANY)

    def f32(*shape):
        return pltpu.VMEM(shape, F32)

    def bf16(*shape):
        return pltpu.VMEM(shape, BF16)

    dma = pltpu.SemaphoreType.DMA
    layer_out, grad_out, gspec = pl.pallas_call(
        kernel,
        out_shape=[
            jax.ShapeDtypeStruct((512, 8, 256), BF16),
            jax.ShapeDtypeStruct((512, 8, 256), BF16),
            jax.ShapeDtypeStruct((2, 32, 64, 32), F32),
        ],
        in_specs=[vmem, hbm, vmem, hbm, vmem, vmem, hbm, vmem, vmem, vmem, hbm, hbm, hbm, hbm, vmem, vmem, hbm, hbm, vmem, vmem],
        out_specs=[vmem, vmem, vmem],
        scratch_shapes=[
            f32(2, 4096, 128), f32(2, 4096, 128), f32(2, 4096, 128),
            bf16(8, 512, 256), bf16(8, 512, 256), bf16(8, 512, 256),
            bf16(512, 8, 256), f32(2, 32, 64, 32), f32(2, 64, 64, 64),
            f32(256, 512), f32(256, 512), f32(256, 256), f32(128, 256),
            f32(512, 256), f32(512, 256), f32(2, 8, 1024), f32(16, 512),
            bf16(256, 1024), bf16(256, 1024), bf16(1024, 512), bf16(1024, 512),
            bf16(80, 256), bf16(128, 256), bf16(2, 256, 512), bf16(2, 256, 512), bf16(2, 256, 256), bf16(2, 128, 256),
            bf16(2, 512, 256), bf16(2, 512, 256),
            bf16(512, 512), bf16(512, 512), f32(256, 256), f32(2, 128, 256), f32(128, 128), f32(2, 64, 32),
            f32(2, 2, 2, PAIRS, 128), f32(2, 2, 512, 128), f32(2, 2, 512, 128), f32(2, 16, 8, 256), f32(2, 16, 8, 256),
            f32(2, 2, 8, 256), f32(2, 16, 8, 256), f32(2, 2, 512, 128), f32(2, 2, 512, 128), f32(2, 2, 2, PAIRS, 128),
            f32(256, 128), f32(256, 128), f32(8, 8, 512), f32(8, 8, 512), f32(8, 1024), f32(8, 8, 1024),
            f32(256, 128), f32(256, 128),
            dma((11,)), dma((4,)), dma((4,)), dma((4,)), dma((4,)), dma((4,)), dma((4,)), dma((4,)),
            dma((4,)), dma((4,)),
        ],
        compiler_params=pltpu.CompilerParams(
            collective_id=0, has_side_effects=True, vmem_limit_bytes=60 * 1024 * 1024
        ),
        name="fno_layer",
    )(
        features.reshape(512, 8, 256), cotangent.reshape(512, 8, 256), pointwise_fine, fine, lift_weight,
        pointwise_coarse, coarse, project_weight.T,
        table["tx"], table["ix"], table["ty"], table["zf"], table["zi"], table["ti"], table["txc"], table["tyc"],
        table["zfc"], table["zic"], table["tic"], table["ixc"],
    )
    shape = (32, 16, 8, 256)
    gspec = gspec.reshape(2, 32, 16, 1, 4, 32).transpose(0, 1, 5, 2, 3, 4)
    return layer_out.reshape(shape), grad_out.reshape(shape), gspec


def solution(mesh):
    placed = (
        P(None, "py", "px", None),
        P(None, "py", "px", None),
        P(),
        P(None, None, None, None, "px", "py"),
        P(),
        P(),
        P(None, None, None, None, "px", "py"),
        P(),
    )
    return jax.shard_map(
        body,
        mesh=mesh,
        in_specs=placed,
        out_specs=(
            P(None, "py", "px", None),
            P(None, "py", "px", None),
            P(None, None, None, None, "px", "py"),
        ),
        check_vma=False,
    )
```

profile of v0, /device:TPU:1, one launch (start us, length us, event | category | flops | bytes accessed | tf_op | source)
XLA Modules:
  0.0 127.9 jit_solution(14945337183745667633)
XLA Ops:
  0.6 120.3 %fno_layer.1 = (bf16[512,8,256]{2,1,0:T(8,128)(2,1)}, bf16[512,8,256]{2,1,0:T(8,128)(2,1)}, f32[2,32,64,32]{3,2,1,0:T(8,128)}) custom-call(bf16[512,8,256]{2,1,0:T(8,128)(2,1)} %bitcast.20, bf16[512,8,256]{2,1,0:T(8,128)(2,1)} %bitcast.21, bf16[32,32]{1,0:T(8,128)(2,1)} %w_fine.1, f32[2,32,64,32]{3,2,1,0:T(8,128)} %bitcast.22, bf16[32,64]{1,0:T(8,128)(2,1)} %lift.1, ...), custom_call_target="tpu_custom_call" | custom-call | tf_op jit(solution)/shard_map/fno_layer/pallas_call | solution.py:800
  120.9 0.0 copy-start.1
  120.9 3.3 %copy.27 = bf16[32,16,8,256]{3,2,1,0:T(8,128)(2,1)} copy(bf16[32,16,8,256]{3,2,1,0:T(8,128)(2,1)} %bitcast.19) | data formatting | bytes 4194304
  124.2 0.0 copy-done.1
  124.2 0.0 copy-start
  124.2 1.3 %copy.28 = bf16[32,16,8,256]{3,2,1,0:T(8,128)(2,1)} copy(bf16[32,16,8,256]{3,2,1,0:T(8,128)(2,1)S(1)} %bitcast.18) | data formatting | bytes 4194304
  125.5 1.0 copy-done
  126.6 1.3 %copy.29 = f32[2,32,32,16,1,4]{2,5,4,3,1,0:T(4,128)} copy(f32[2,32,32,16,1,4]{2,5,4,3,1,0:T(4,128)S(1)} %bitcast.17) | data formatting | bytes 1048576
Async XLA Ops:
  120.9 3.3 %copy-start.1 = (bf16[512,8,256]{2,1,0:T(8,128)(2,1)S(1)}, bf16[512,8,256]{2,1,0:T(8,128)(2,1)}, u32[]{:S(2)}) copy-start(bf16[512,8,256]{2,1,0:T(8,128)(2,1)} %get-tuple-element.7) | copy-start | bytes 6291460
  124.2 2.3 %copy-start = (f32[2,32,64,32]{3,2,1,0:T(8,128)S(1)}, f32[2,32,64,32]{3,2,1,0:T(8,128)}, u32[]{:S(2)}) copy-start(f32[2,32,64,32]{3,2,1,0:T(8,128)} %get-tuple-element.8) | copy-start | bytes 1572868
where the time goes:
time: 128 us
  Pallas kernels  120 us (94%)
  local copies, waits for them, and re-layouts  6.95 us (5%)
    pallas_call x1, Pallas kernels, body(): pl.pallas_call(kernel, out_shape=[jax.ShapeDtypeStruct((512, 8, 256), BF1...  120 us
    unnamed x7, local copies, waits for them, and re-layouts  6.95 us

commit v1 on v0

--- a/solution.py
+++ b/solution.py
@@ -234,22 +234,35 @@
     return jnp.where(iota((64, 1), 0) < 4, 1.0 / cells, 2.0 / cells).astype(F32)
 
 
+def stacked_table(table):
+    high, low = split(table)
+    high, low = high.astype(F32), low.astype(F32)
+    return jnp.concatenate([high, high, low, jnp.zeros((8, 256), F32)], axis=0).astype(BF16)
+
+
+def synthesise_x(value, table):
+    high = value.astype(BF16).astype(F32)
+    pad = jnp.zeros((8, value.shape[1]), F32)
+    stacked = jnp.concatenate([high, value - high, high, pad], axis=0)
+    return dot(stacked.T.astype(BF16), table)
+
+
 def tanh_gelu(value):
     return 0.5 * value * (1.0 + jnp.tanh(ROOT * (value + 0.044715 * value * value * value)))
 
 
 def kernel(
-    feat, cot_hbm, w_fine, spec_hbm, lift, w_coarse, spec_c_hbm, project,
+    feat_hbm, cot_hbm, w_fine, spec_hbm, lift, w_coarse, spec_c_hbm, project,
     tx_in, ix_in, ty_hbm, zf_hbm, zi_hbm, ti_hbm, txc_in, tyc_in, zfc_hbm, zic_hbm, tic_in, ixc_in,
-    layer_out, grad_out, gspec,
-    b0, b1, b2, fy, gph, gpl, cot, spec, spec_c,
+    layer_hbm, dir_hbm, gspec_hbm, g_hbm,
+    b0, b1, b2, fy, gph, gpl, feat, cot, spec, spec_c, layer_out, gspec,
     ty, tye, zf, zi, ti, tie, zfc, zic, zfull_h, zfull_l, zifull_h, zifull_l,
     tx, ix, ty_s, tye_s, zf_s, zi_s, ti_s, tie_s,
     wk, wkt, yc, rst, rst2, modes,
     s_buf, rx, rxe, ex, re_buf, hq, ri, sv, sve, g_buf,
     sc, rc, exc, rec, hc, ric, svc, gc,
-    load_sem, px_send, px_recv, pxe_send, pxe_recv, py_send, py_recv, pye_send,
-    c_send, c_recv,
+    load_sem, out_sem, px_send, px_recv, pxe_send, pxe_recv, py_send, py_recv, pye_send,
+    c_send, c_recv, here,
 ):
     me = lax.axis_index("px")
     mine = lax.axis_index("py")
@@ -261,7 +274,7 @@
     regular = 1 - is0 - is16
 
     loads = [
-        (cot_hbm, cot), (spec_hbm, spec), (spec_c_hbm, spec_c),
+        (feat_hbm, feat), (cot_hbm, cot), (spec_hbm, spec), (spec_c_hbm, spec_c),
         (ty_hbm.at[kind], ty), (ty_hbm.at[4], tye), (zf_hbm.at[mine], zf), (zi_hbm.at[mine], zi),
         (ti_hbm.at[kind], ti), (ti_hbm.at[4], tie), (zfc_hbm.at[mine], zfc), (zic_hbm.at[mine], zic),
     ]
@@ -270,118 +283,104 @@
         load.start()
 
     barrier = pltpu.get_barrier_semaphore()
-
-    def greet(t, carry):
-        pl.semaphore_signal(
-            barrier, inc=1, device_id={"px": lax.rem(me + t, NPX), "py": mine}, device_id_type=MESH
-        )
-        return carry
-
-    lax.fori_loop(1, NPX, greet, 0)
-
-    def greet_own(t, carry):
-        pl.semaphore_signal(
-            barrier, inc=1, device_id={"px": me, "py": lax.rem(mine + t, NPY)}, device_id_type=MESH
-        )
-        return carry
-
-    lax.fori_loop(1, NPY, greet_own, 0)
-
-    @pl.when(regular == 1)
-    def _():
-        def greet_partner(t, carry):
-            pl.semaphore_signal(
-                barrier, inc=1, device_id={"px": partner, "py": lax.rem(mine + t, NPY)},
-                device_id_type=MESH,
-            )
-            return carry
-
-        lax.fori_loop(1, NPY, greet_partner, 0)
+    row = 8 * lax.div(me, 8)
+
+    def tell(semaphore, px, py):
+        pl.semaphore_signal(semaphore, inc=1, device_id={"px": px, "py": py}, device_id_type=MESH)
+
+    for t in range(1, 8):
+        tell(barrier, row + lax.rem(me + t, 8), mine)
+    for t in range(1, 4):
+        tell(barrier, lax.rem(me + 8 * t, NPX), mine)
+    for t in range(1, 4):
+        tell(barrier, me, lax.rem(mine + 2 * t, NPY))
+    other = 2 * lax.div(mine, 2) + 1 - lax.rem(mine, 2)
+    tell(barrier, me, other)
+    pl.semaphore_wait(barrier, 14)
+    for t in range(1, 4):
+        tell(here.at[0], lax.rem(me + 8 * t, NPX), mine)
 
     def pair_row(d):
         h = lax.div(d + 15, 32)
         return h, pl.multiple_of(16 * (d * (1 - 2 * h) + 32 * h), 16)
 
-    def px_forward(n):
-        def send(t, carry):
-            d = lax.rem(me + t, NPX)
+    def at16(d):
+        return pl.ds(pl.multiple_of(16 * d, 16), 16)
+
+    def px_forward(n, t):
+        k = 4 * n + t
+
+        def send(step, carry):
+            d = lax.rem(me + step, NPX)
             h, row = pair_row(d)
             pltpu.make_async_remote_copy(
-                s_buf.at[n, h, :, pl.ds(row, 16)], rx.at[n, :, pl.ds(pl.multiple_of(16 * me, 16), 16)],
-                px_send.at[2 * n], px_recv.at[2 * n], device_id={"px": d, "py": mine}, device_id_type=MESH,
+                s_buf.at[n, t, h, pl.ds(row, 16)], rx.at[n, t, at16(me)],
+                px_send.at[k], px_recv.at[k], device_id={"px": d, "py": mine}, device_id_type=MESH,
             ).start()
             return carry
 
         lax.fori_loop(1, NPX, send, 0)
         h, row = pair_row(me)
-        pltpu.make_async_copy(
-            s_buf.at[n, h, :, pl.ds(row, 16)], rx.at[n, :, pl.ds(pl.multiple_of(16 * me, 16), 16)], px_recv.at[2 * n]
-        ).start()
+        pltpu.make_async_copy(s_buf.at[n, t, h, pl.ds(row, 16)], rx.at[n, t, at16(me)], px_recv.at[k]).start()
 
         @pl.when(is16 == 0)
         def _():
             pltpu.make_async_remote_copy(
-                s_buf.at[n, 1, :, pl.ds(256, 16)], rxe.at[n, :, pl.ds(pl.multiple_of(16 * me, 16), 16)],
-                pxe_send.at[2 * n], pxe_recv.at[2 * n], device_id={"px": 16, "py": mine}, device_id_type=MESH,
+                s_buf.at[n, t, 1, pl.ds(256, 16)], rxe.at[n, t, at16(me)],
+                pxe_send.at[k], pxe_recv.at[k], device_id={"px": 16, "py": mine}, device_id_type=MESH,
             ).start()
 
         @pl.when(is16 == 1)
         def _():
             pltpu.make_async_copy(
-                s_buf.at[n, 1, :, pl.ds(256, 16)], rxe.at[n, :, pl.ds(pl.multiple_of(16 * me, 16), 16)],
-                pxe_recv.at[2 * n],
+                s_buf.at[n, t, 1, pl.ds(256, 16)], rxe.at[n, t, at16(me)], pxe_recv.at[k]
             ).start()
 
-    def px_forward_wait(n):
-        pltpu.make_async_copy(rx.at[n], rx.at[n], px_recv.at[2 * n]).wait()
+    def px_forward_wait(n, t):
+        k = 4 * n + t
+        pltpu.make_async_copy(rx.at[n, t], rx.at[n, t], px_recv.at[k]).wait()
 
         @pl.when(is16 == 1)
         def _():
-            pltpu.make_async_copy(rxe.at[n], rxe.at[n], pxe_recv.at[2 * n]).wait()
-
-    def px_inverse(n):
+            pltpu.make_async_copy(rxe.at[n, t], rxe.at[n, t], pxe_recv.at[k]).wait()
+
+    def px_inverse(n, t, target):
+        k = 4 * n + 2 + t
         h, row = pair_row(me)
 
-        def send(t, carry):
-            d = lax.rem(me + t, NPX)
+        def send(step, carry):
+            d = lax.rem(me + step, NPX)
             pltpu.make_async_remote_copy(
-                sv.at[n, :, pl.ds(pl.multiple_of(16 * d, 16), 16)], g_buf.at[n, h, :, pl.ds(row, 16)],
-                px_send.at[2 * n + 1], px_recv.at[2 * n + 1],
-                device_id={"px": d, "py": mine}, device_id_type=MESH,
+                sv.at[n, t, at16(d)], target.at[t, h, pl.ds(row, 16)],
+                px_send.at[k], px_recv.at[k], device_id={"px": d, "py": mine}, device_id_type=MESH,
             ).start()
             return carry
 
         lax.fori_loop(1, NPX, send, 0)
-        pltpu.make_async_copy(
-            sv.at[n, :, pl.ds(pl.multiple_of(16 * me, 16), 16)], g_buf.at[n, h, :, pl.ds(row, 16)],
-            px_recv.at[2 * n + 1],
-        ).start()
+        pltpu.make_async_copy(sv.at[n, t, at16(me)], target.at[t, h, pl.ds(row, 16)], px_recv.at[k]).start()
 
         @pl.when(is16 == 1)
         def _():
-            def send_extra(t, carry):
-                d = lax.rem(me + t, NPX)
+            def send_extra(step, carry):
+                d = lax.rem(me + step, NPX)
                 pltpu.make_async_remote_copy(
-                    sve.at[n, :, pl.ds(pl.multiple_of(16 * d, 16), 16)], g_buf.at[n, 1, :, pl.ds(256, 16)],
-                    pxe_send.at[2 * n + 1], pxe_recv.at[2 * n + 1],
-                    device_id={"px": d, "py": mine}, device_id_type=MESH,
+                    sve.at[n, t, at16(d)], target.at[t, 1, pl.ds(256, 16)],
+                    pxe_send.at[k], pxe_recv.at[k], device_id={"px": d, "py": mine}, device_id_type=MESH,
                 ).start()
                 return carry
 
             lax.fori_loop(1, NPX, send_extra, 0)
-            pltpu.make_async_copy(
-                sve.at[n, :, pl.ds(pl.multiple_of(16 * me, 16), 16)], g_buf.at[n, 1, :, pl.ds(256, 16)],
-                pxe_recv.at[2 * n + 1],
-            ).start()
-
-    def px_inverse_wait(n):
-        pltpu.make_async_copy(rx.at[n], rx.at[n], px_recv.at[2 * n + 1]).wait()
-        some = g_buf.at[n, 1, :, pl.ds(256, 16)]
-        pltpu.make_async_copy(some, some, pxe_recv.at[2 * n + 1]).wait()
+            pltpu.make_async_copy(sve.at[n, t, at16(me)], target.at[t, 1, pl.ds(256, 16)], pxe_recv.at[k]).start()
+
+    def px_inverse_wait(n, t):
+        k = 4 * n + 2 + t
+        pltpu.make_async_copy(rx.at[n, t], rx.at[n, t], px_recv.at[k]).wait()
+        some = rx.at[n, t, pl.ds(0, 16)]
+        pltpu.make_async_copy(some, some, pxe_recv.at[k]).wait()
 
     def py_exchange(slot, source, target):
-        def send(t, carry):
-            p = lax.rem(mine + t, NPY)
+        def send(step, carry):
+            p = lax.rem(mine + step, NPY)
             for q, to in ((0, me), (1, partner)):
                 pltpu.make_async_remote_copy(
                     source(q, p), target.at[8 * q + mine], py_send.at[slot], py_recv.at[slot],
@@ -435,95 +434,78 @@
     def coarse_wait(slot, target):
         pltpu.make_async_copy(target, target, c_recv.at[slot]).wait()
 
-    def tiles(ref, n):
-        return jnp.concatenate([ref[n, 0], ref[n, 1]], axis=1)
-
-    def put_tiles(ref, n, value):
-        ref[n, 0] = value[:, :128]
-        ref[n, 1] = value[:, 128:]
-
-    def store_pairs(n, y, both):
-        for h in range(2):
-            for t in range(2):
-                at = 256 * h + 128 * t
-                s_buf[n, h, t, pl.ds(y, 40, stride=8), :] = both[:, at : at + 128]
-
-    def fix_zero(n):
-        s_buf[n, 0, :, pl.ds(8, 8), :] = s_buf[n, 1, :, pl.ds(0, 8), :]
-
-    def forward_yz(n):
-        high, low = split(tiles(rx, n))
+    def fix_zero(n, t):
+        s_buf[n, t, 0, pl.ds(8, 8), :] = s_buf[n, t, 1, pl.ds(0, 8), :]
+
+    def forward_yz(n, t):
+        high, low = split(rx[n, t])
         yc[...] = dot3(ty_s[0], ty_s[1], high, low)
 
         @pl.when(is16 == 1)
         def _():
-            high, low = split(tiles(rxe, n))
+            high, low = split(rxe[n, t])
             yc[...] += dot3(tye_s[0], tye_s[1], high, low)
 
         dup = ((iota((128, 128), 0) >> 2) & 1) == 0
-        for t in range(2):
-            lanes = pl.ds(128 * t, 128)
-            both = jnp.concatenate([yc[pl.ds(0, 128), lanes], yc[pl.ds(128, 128), lanes]], axis=1)
-            high, low = split(both)
-            full = dot3(high, low, zf_s[0], zf_s[1])
-            picked = jnp.where(dup, full[:, :128], full[:, 128:])
-            ex[n, :, :, lanes] = picked.reshape(16, 8, 128)
+        both = jnp.concatenate([yc[pl.ds(0, 128), :], yc[pl.ds(128, 128), :]], axis=1)
+        high, low = split(both)
+        full = dot3(high, low, zf_s[0], zf_s[1])
+        ex[n, t] = jnp.where(dup, full[:, :128], full[:, 128:]).reshape(16, 8, 128)
+        py_exchange(4 * n + t, lambda q, p: ex.at[n, t, 8 * q + p], re_buf.at[n, t])
 
     def gather_modes(n):
-        slot0 = jnp.sum(re_buf[n, 0:8], axis=0)
-        slot1 = jnp.sum(re_buf[n, 8:16], axis=0)
+        slots = []
+        for q in range(2):
+            parts = []
+            for t in range(2):
+                if q == 0:
+                    py_wait(4 * n + t, re_buf.at[n, t])
+                parts.append(jnp.sum(re_buf[n, t, 8 * q : 8 * q + 8], axis=0))
+            slots.append(jnp.concatenate(parts, axis=1))
         swap = upper == 1
-        first = jnp.where(swap, slot1, slot0)
-        second = jnp.where(swap, slot0, slot1)
+        first = jnp.where(swap, slots[1], slots[0])
+        second = jnp.where(swap, slots[0], slots[1])
         return to_modes(jnp.concatenate([first, second], axis=1), 32)
 
     def spread_modes(n, real, imag):
         packed = from_modes(real, imag, 32)
-        first, second = packed[:, :256], packed[:, 256:]
         swap = upper == 1
-        hq[n, 0] = jnp.where(swap, second, first)
-        hq[n, 1] = jnp.where(swap, first, second)
-
-    def inverse_zy(n):
-        value = ri[n].reshape(128, 256)
-        parts = []
         for t in range(2):
-            high, low = split(value[:, 128 * t : 128 * t + 128])
-            parts.append(dot3(high, low, zi_s[0], zi_s[1]))
-        stacked = jnp.concatenate(
+            first, second = packed[:, 128 * t : 128 * t + 128], packed[:, 256 + 128 * t : 384 + 128 * t]
+            hq[n, t, 0] = jnp.where(swap, second, first)
+            hq[n, t, 1] = jnp.where(swap, first, second)
+            py_exchange(4 * n + 2 + t, lambda q, p: hq.at[n, t, q], ri.at[n, t])
+
+    def inverse_zy(n, t, target):
+        py_wait(4 * n + 2 + t, ri.at[n, t])
+        high, low = split(ri[n, t].reshape(128, 128))
+        full = dot3(high, low, zi_s[0], zi_s[1])
+        high, low = split(jnp.concatenate([full[:, :128], full[:, 128:]], axis=0))
+        sv[n, t] = dot3(ti_s[0], ti_s[1], high, low)
+
+        @pl.when(is16 == 1)
+        def _():
+            sve[n, t] = dot3(tie_s[0], tie_s[1], high, low)
+
+        px_inverse(n, t, target)
+
+    def rows_at(h, t):
+        return 256 * h + 128 * t
+
+    def take(ref, t, y):
+        return jnp.concatenate(
             [
-                jnp.concatenate([parts[0][:, :128], parts[1][:, :128]], axis=1),
-                jnp.concatenate([parts[0][:, 128:], parts[1][:, 128:]], axis=1),
+                jnp.concatenate(
+                    [ref[lane, pl.ds(8 * rows_at(h, t) + y, 128, stride=8), :] for lane in range(2)], axis=1
+                )
+                for h in range(2)
             ],
             axis=0,
         )
-        high, low = split(stacked)
-        put_tiles(sv, n, dot3(ti_s[0], ti_s[1], high, low))
-
-        @pl.when(is16 == 1)
-        def _():
-            put_tiles(sve, n, dot3(tie_s[0], tie_s[1], high, low))
-
-    def inverse_x(n, y):
-        parts = [
-            g_buf[n, h, t, pl.ds(y, 40, stride=8), :] for h in range(2) for t in range(2)
-        ]
-        value = jnp.concatenate(parts, axis=1)
-        high = value.astype(BF16).astype(F32)
-        stacked = jnp.concatenate([high, value - high, high, jnp.zeros((8, 512), F32)], axis=0)
-        return dot(stacked.T.astype(BF16), ix[...])
-
-    def fix_inverse_zero(n):
-        g_buf[n, 1, :, pl.ds(0, 8), :] = g_buf[n, 0, :, pl.ds(8, 8), :]
-
-    def take(ref, y):
-        return jnp.concatenate(
-            [ref[t, pl.ds(y, 512, stride=8), :] for t in range(2)], axis=1
-        )
 
     def put(ref, y, value):
-        for t in range(2):
-            ref[t, pl.ds(y, 512, stride=8), :] = value[:, 128 * t : 128 * t + 128]
+        for lane in range(2):
+            ref[lane, pl.ds(y, 512, stride=8), :] = value[:, 128 * lane : 128 * lane + 128]
 
     def block(ref, y):
         rows = pl.ds(pl.multiple_of(512 * y, 512), 512)
@@ -534,37 +516,66 @@
         ref[0, rows, :] = value[:, :128]
         ref[1, rows, :] = value[:, 128:]
 
-    def unpack(ref, field):
-        for t in range(2):
-            ref[t] = field[:, :, pl.ds(128 * t, 128)].astype(F32).reshape(4096, 128)
+    def part_rows(h, t, y):
+        return pl.ds(pl.multiple_of(512 * y + rows_at(h, t), 128), 128)
+
+    def some_rows(ref, t, y):
+        return jnp.concatenate(
+            [
+                jnp.concatenate([ref[lane, part_rows(h, t, y), :] for lane in range(2)], axis=1)
+                for h in range(2)
+            ],
+            axis=0,
+        )
+
+    def put_part(ref, t, y, value):
+        for h in range(2):
+            for lane in range(2):
+                ref[lane, part_rows(h, t, y), :] = value[128 * h : 128 * h + 128, 128 * lane : 128 * lane + 128]
+
+    def put_rows(ref, t, y, value):
+        for h in range(2):
+            ref[y, pl.ds(rows_at(h, t), 128), :] = value[128 * h : 128 * h + 128]
+
+    def unpack(ref, field, t):
+        for h in range(2):
+            for lane in range(2):
+                some = field[pl.ds(rows_at(h, t), 128), :, pl.ds(128 * lane, 128)]
+                ref[lane, pl.ds(8 * rows_at(h, t), 1024), :] = some.astype(F32).reshape(1024, 128)
 
     def pack(field, ref):
-        for t in range(2):
-            field[:, :, pl.ds(128 * t, 128)] = ref[t].reshape(512, 8, 128).astype(BF16)
+        for lane in range(2):
+            field[:, :, pl.ds(128 * lane, 128)] = ref[lane].reshape(512, 8, 128).astype(BF16)
+
+    def store_pairs(n, t, y, both):
+        for h in range(2):
+            s_buf[n, t, h, pl.ds(y, 40, stride=8), :] = both[:, 128 * h : 128 * h + 128]
 
     high, low = split(tx_in[...])
     tx[pl.ds(0, 40), :] = high
     tx[pl.ds(40, 40), :] = low
-    high, low = split(ix_in[...])
-    ix[...] = jnp.concatenate([high.astype(F32), high.astype(F32), low.astype(F32), jnp.zeros((8, 256), F32)], axis=0).astype(BF16)
-    unpack(b0, feat)
-
-    def analyse_x(y, carry):
-        field = take(b0, y).astype(BF16)
-        fy[y] = field
-        both = dot(tx[...], field, ((1,), (1,)))
-        store_pairs(0, y, both[:40] + both[40:])
-        return carry
-
-    lax.fori_loop(0, 8, analyse_x, 0)
-    fix_zero(0)
-    for n in range(2):
-        g_buf[n, :, :, pl.ds(272, 48), :] = jnp.zeros((2, 2, 48, 128), F32)
-        g_buf[n, 1, :, pl.ds(0, 16), :] = jnp.zeros((2, 16, 128), F32)
+    ix[...] = stacked_table(ix_in[...])
+    loads[0].wait()
+    for t in range(2):
+        unpack(b0, feat, t)
+
+        def analyse_x(y, carry):
+            field = take(b0, t, y).astype(BF16)
+            put_rows(fy, t, y, field)
+            both = dot(tx[...], field, ((1,), (1,)))
+            store_pairs(0, t, y, both[:40] + both[40:])
+            return carry
+
+        lax.fori_loop(0, 8, analyse_x, 0)
+        fix_zero(0, t)
+        if t == 0:
+            pl.semaphore_wait(here.at[0], 3)
+        px_forward(0, t)
+    for t in range(1, 4):
+        tell(here.at[1], me, lax.rem(mine + 2 * t, NPY))
+    g_buf[:, :, pl.ds(272, 48), :] = jnp.zeros((2, 2, 48, 128), F32)
+    g_buf[:, 1, pl.ds(0, 16), :] = jnp.zeros((2, 16, 128), F32)
     sc[...] = jnp.zeros((256, 128), F32)
-
-    pl.semaphore_wait(barrier, 38 + 7 * regular)
-    px_forward(0)
 
     txc_high, txc_low = split(txc_in[...])
     pool = ones_where(iota((128, 512), 0) == (iota((128, 512), 1) >> 2))
@@ -579,6 +590,9 @@
         sc[pl.ds(big, 64, stride=4), :] = part
     coarse_px(0, sc, rc)
 
+    pl.semaphore_wait(here.at[1], 3)
+    tell(here.at[2], me, other)
+
     wk[...] = kron_eye(rows_of(w_fine[...], 32, 4, 1), 4)
     wkt[...] = kron_eye(rows_of(w_fine[...], 32, 4, 0), 4)
 
@@ -587,15 +601,16 @@
         return carry
 
     lax.fori_loop(0, 8, local, 0)
-    loads[0].wait()
-    unpack(b1, cot)
+    loads[1].wait()
+    for t in range(2):
+        unpack(b1, cot, t)
     low_total = jnp.zeros((128, 128), F32)
     for big in range(2):
         gather = ones_where(iota((256, 128), 1) == 64 * big + (iota((256, 128), 0) >> 2))
         high, low = split(rst[big])
         low_total = low_total + dot(high, gather) + dot(low, gather)
     rst2[...] = low_total
-    for n in range(1, 11):
+    for n in range(2, 12):
         loads[n].wait()
     for whole, parts in ((ty, ty_s), (tye, tye_s), (zf, zf_s), (zi, zi_s), (ti, ti_s), (tie, tie_s)):
         high, low = split(whole[...])
@@ -619,9 +634,10 @@
 
     lax.fori_loop(0, 8, build, 0)
 
-    px_forward_wait(0)
-    forward_yz(0)
-    py_exchange(0, lambda q, p: ex.at[0, 8 * q + p], re_buf.at[0])
+    pl.semaphore_wait(here.at[2], 1)
+    for t in range(2):
+        px_forward_wait(0, t)
+        forward_yz(0, t)
 
     coarse_wait(0, rc)
     high, low = split(rc[...])
@@ -632,14 +648,12 @@
     exc[...] = jnp.where(dup, full[:, :512], full[:, 512:]).reshape(8, 8, 512)
     coarse_py(1, lambda p: exc.at[p], rec)
 
-    py_wait(0, re_buf.at[0])
     real, imag = gather_modes(0)
     modes[0] = real
     modes[1] = imag
     out_real, out_imag = mix_modes(spec, real, imag, 32)
     fine_factor = mode_factor(256.0 * 256.0 * 128.0)
     spread_modes(0, out_real * fine_factor, out_imag * fine_factor)
-    py_exchange(1, lambda q, p: hq.at[0, q], ri.at[0])
 
     coarse_wait(1, rec)
     real, imag = to_modes(jnp.sum(rec[...], axis=0), 32)
@@ -650,9 +664,8 @@
     hc[...] = from_modes(out_real * coarse_factor, out_imag * coarse_factor, 64)
     coarse_py(2, lambda p: hc, ric)
 
-    py_wait(1, ri.at[0])
-    inverse_zy(0)
-    px_inverse(0)
+    for t in range(2):
+        inverse_zy(0, t, g_buf)
 
     coarse_wait(2, ric)
     high, low = split(ric[...].reshape(64, 1024))
@@ -663,34 +676,36 @@
         svc[pl.ds(hh, 128, stride=2), :] = along_y[:, 128 * hh : 128 * hh + 128]
     coarse_px(3, svc, gc)
 
-    px_inverse_wait(0)
-    fix_inverse_zero(0)
-
-    def middle(y, carry):
-        pre = block(b2, y) + inverse_x(0, y)
-        square = pre * pre
-        t = jnp.tanh(ROOT * pre * (1.0 + 0.044715 * square))
-        half = 0.5 * (1.0 + t)
-        put_block(b0, y, pre * half)
-        slope = half + 0.5 * pre * (1.0 - t * t) * (ROOT + (3.0 * 0.044715 * ROOT) * square)
-        grad = take(b1, y) * slope
-        high, low = split(grad)
-        gph[y] = high
-        gpl[y] = low
-        both = dot(tx[...], high, ((1,), (1,)))
-        part = both[:40] + both[40:] + dot(tx[pl.ds(0, 40), :], low, ((1,), (1,)))
-        store_pairs(1, y, part)
-        return carry
-
-    lax.fori_loop(0, 8, middle, 0)
-    fix_zero(1)
-    px_forward(1)
+    for t in range(2):
+        px_inverse_wait(0, t)
+        g_buf[t, 1, pl.ds(0, 8), :] = g_buf[t, 0, pl.ds(8, 8), :]
+
+        def middle(y, carry):
+            value = jnp.concatenate([g_buf[t, h, pl.ds(y, 40, stride=8), :] for h in range(2)], axis=1)
+            pre = some_rows(b2, t, y) + synthesise_x(value, ix[...])
+            square = pre * pre
+            tanh = jnp.tanh(ROOT * pre * (1.0 + 0.044715 * square))
+            half = 0.5 * (1.0 + tanh)
+            put_part(b0, t, y, pre * half)
+            slope = half + 0.5 * pre * (1.0 - tanh * tanh) * (ROOT + (3.0 * 0.044715 * ROOT) * square)
+            high, low = split(take(b1, t, y) * slope)
+            put_rows(gph, t, y, high)
+            put_rows(gpl, t, y, low)
+            both = dot(tx[...], high, ((1,), (1,)))
+            store_pairs(1, t, y, both[:40] + both[40:] + dot(tx[pl.ds(0, 40), :], low, ((1,), (1,))))
+            return carry
+
+        lax.fori_loop(0, 8, middle, 0)
+        fix_zero(1, t)
+        px_forward(1, t)
 
     def direct(y, carry):
         put_block(b1, y, dot(wkt[...], gph[y]) + dot(wkt[...], gpl[y]))
         return carry
 
     lax.fori_loop(0, 8, direct, 0)
+    writes = [pltpu.make_async_copy(b1, dir_hbm, out_sem.at[0])]
+    writes[0].start()
 
     coarse_wait(3, gc)
     halves_out = []
@@ -717,11 +732,12 @@
             y = 4 * big + small
             put(b2, y, block(b0, y) + prolonged)
     pack(layer_out, b2)
-
-    px_forward_wait(1)
-    forward_yz(1)
-    py_exchange(2, lambda q, p: ex.at[1, 8 * q + p], re_buf.at[1])
-    py_wait(2, re_buf.at[1])
+    writes.append(pltpu.make_async_copy(layer_out, layer_hbm, out_sem.at[1]))
+    writes[1].start()
+
+    for t in range(2):
+        px_forward_wait(1, t)
+        forward_yz(1, t)
     real, imag = gather_modes(1)
     real, imag = real * fine_factor, imag * fine_factor
     lane = iota((64, 32), 1)
@@ -734,50 +750,65 @@
         pull_real = jnp.where(lane == i, a, pull_real)
         pull_imag = jnp.where(lane == i, b, pull_imag)
     spread_modes(1, pull_real, pull_imag)
-    py_exchange(3, lambda q, p: hq.at[1, q], ri.at[1])
     x_real, x_imag = modes[0], modes[1]
     for i in range(32):
         a, b = column(x_real, i), column(x_imag, i)
         gspec[0, i] = real * a + imag * b
         gspec[1, i] = imag * a - real * b
-    py_wait(3, ri.at[1])
-    inverse_zy(1)
-    px_inverse(1)
-
-    px_inverse_wait(1)
-    fix_inverse_zero(1)
-
-    def final(y, carry):
-        put(b2, y, block(b1, y) + inverse_x(1, y))
-        return carry
-
-    lax.fori_loop(0, 8, final, 0)
-    pack(grad_out, b2)
-
-    for n in range(2):
-        most = rx.at[n, :, pl.ds(0, 496)]
-        for k in range(2):
-            pltpu.make_async_copy(most, most, px_send.at[2 * n + k]).wait()
-
-        @pl.when(is16 == 0)
-        def _():
-            some = rx.at[n, :, pl.ds(0, 16)]
-            pltpu.make_async_copy(some, some, pxe_send.at[2 * n]).wait()
-
-        @pl.when(is16 == 1)
-        def _():
-            pltpu.make_async_copy(most, most, pxe_send.at[2 * n + 1]).wait()
-
-    for slot in range(4):
-        most = ex.at[0, pl.ds(0, 14)]
-        pltpu.make_async_copy(most, most, py_send.at[slot]).wait()
+    writes.append(pltpu.make_async_copy(gspec, gspec_hbm, out_sem.at[2]))
+    writes[2].start()
+    for t in range(2):
+        inverse_zy(1, t, g_hbm)
+    for t in range(2):
+        px_inverse_wait(1, t)
+
+    for write in writes:
+        write.wait()
+    for k in range(8):
+        most = rx.at[0, 0, pl.ds(0, 496)]
+        pltpu.make_async_copy(most, most, px_send.at[k]).wait()
+        if k % 4 < 2:
+
+            @pl.when(is16 == 0)
+            def _():
+                some = rx.at[0, 0, pl.ds(0, 16)]
+                pltpu.make_async_copy(some, some, pxe_send.at[k]).wait()
+
+        else:
+
+            @pl.when(is16 == 1)
+            def _():
+                pltpu.make_async_copy(most, most, pxe_send.at[k]).wait()
+
+    for slot in range(8):
+        some = ex.at[0, 0, pl.ds(0, 14)]
+        pltpu.make_async_copy(some, some, py_send.at[slot]).wait()
 
         @pl.when(regular == 1)
         def _():
-            pltpu.make_async_copy(ex.at[0, 0], ex.at[0, 0], pye_send.at[slot]).wait()
+            pltpu.make_async_copy(ex.at[0, 0, 0], ex.at[0, 0, 0], pye_send.at[slot]).wait()
 
     for slot, most in ((0, rc.at[pl.ds(0, 248)]), (1, exc.at[pl.ds(0, 7)]), (2, ric.at[pl.ds(0, 7)]), (3, gc.at[pl.ds(0, 248)])):
         pltpu.make_async_copy(most, most, c_send.at[slot]).wait()
+
+
+def finish(g_ref, zero_ref, dir_ref, layer_ref, gspec_ref, ix_in, layer_out, grad_out, gspec_out, kept, mixed):
+    second = pl.program_id(0) >= 2
+    rows = iota((PAIRS, 128), 0)
+    value = jnp.where(rows < 272, g_ref[0, 0], 0.0)
+    zero = jnp.concatenate([zero_ref[0, 0], jnp.zeros((PAIRS - 8, 128), F32)], axis=0)
+    kept[...] = jnp.where(jnp.logical_and(second, rows < 16), zero, value)
+    table = stacked_table(ix_in[...])
+
+    for y in range(8):
+        some = synthesise_x(kept[pl.ds(y, 40, stride=8), :], table)
+        for lane in range(2):
+            at = slice(128 * lane, 128 * lane + 128)
+            mixed[lane, pl.ds(y, 128, stride=8), :] = some[:, at] + dir_ref[lane, y]
+    for lane in range(2):
+        grad_out[:, :, pl.ds(128 * lane, 128)] = mixed[lane].reshape(128, 8, 128).astype(BF16)
+    layer_out[...] = layer_ref[...]
+    gspec_out[...] = gspec_ref[...]
 
 
 def body(
@@ -797,31 +828,33 @@
         return pltpu.VMEM(shape, BF16)
 
     dma = pltpu.SemaphoreType.DMA
-    layer_out, grad_out, gspec = pl.pallas_call(
+    layer, direct, gspec, spectrum = pl.pallas_call(
         kernel,
         out_shape=[
             jax.ShapeDtypeStruct((512, 8, 256), BF16),
-            jax.ShapeDtypeStruct((512, 8, 256), BF16),
+            jax.ShapeDtypeStruct((2, 4096, 128), F32),
             jax.ShapeDtypeStruct((2, 32, 64, 32), F32),
+            jax.ShapeDtypeStruct((2, 2, PAIRS, 128), F32),
         ],
-        in_specs=[vmem, hbm, vmem, hbm, vmem, vmem, hbm, vmem, vmem, vmem, hbm, hbm, hbm, hbm, vmem, vmem, hbm, hbm, vmem, vmem],
-        out_specs=[vmem, vmem, vmem],
+        in_specs=[hbm, hbm, vmem, hbm, vmem, vmem, hbm, vmem, vmem, vmem, hbm, hbm, hbm, hbm, vmem, vmem, hbm, hbm, vmem, vmem],
+        out_specs=[hbm] * 4,
         scratch_shapes=[
             f32(2, 4096, 128), f32(2, 4096, 128), f32(2, 4096, 128),
             bf16(8, 512, 256), bf16(8, 512, 256), bf16(8, 512, 256),
-            bf16(512, 8, 256), f32(2, 32, 64, 32), f32(2, 64, 64, 64),
+            bf16(512, 8, 256), bf16(512, 8, 256), f32(2, 32, 64, 32), f32(2, 64, 64, 64),
+            bf16(512, 8, 256), f32(2, 32, 64, 32),
             f32(256, 512), f32(256, 512), f32(256, 256), f32(128, 256),
             f32(512, 256), f32(512, 256), f32(2, 8, 1024), f32(16, 512),
             bf16(256, 1024), bf16(256, 1024), bf16(1024, 512), bf16(1024, 512),
             bf16(80, 256), bf16(128, 256), bf16(2, 256, 512), bf16(2, 256, 512), bf16(2, 256, 256), bf16(2, 128, 256),
             bf16(2, 512, 256), bf16(2, 512, 256),
-            bf16(512, 512), bf16(512, 512), f32(256, 256), f32(2, 128, 256), f32(128, 128), f32(2, 64, 32),
-            f32(2, 2, 2, PAIRS, 128), f32(2, 2, 512, 128), f32(2, 2, 512, 128), f32(2, 16, 8, 256), f32(2, 16, 8, 256),
-            f32(2, 2, 8, 256), f32(2, 16, 8, 256), f32(2, 2, 512, 128), f32(2, 2, 512, 128), f32(2, 2, 2, PAIRS, 128),
+            bf16(512, 512), bf16(512, 512), f32(256, 128), f32(2, 128, 256), f32(128, 128), f32(2, 64, 32),
+            f32(2, 2, 2, PAIRS, 128), f32(2, 2, 512, 128), f32(2, 2, 512, 128), f32(2, 2, 16, 8, 128), f32(2, 2, 16, 8, 128),
+            f32(2, 2, 2, 8, 128), f32(2, 2, 16, 8, 128), f32(2, 2, 512, 128), f32(2, 2, 512, 128), f32(2, 2, PAIRS, 128),
             f32(256, 128), f32(256, 128), f32(8, 8, 512), f32(8, 8, 512), f32(8, 1024), f32(8, 8, 1024),
             f32(256, 128), f32(256, 128),
-            dma((11,)), dma((4,)), dma((4,)), dma((4,)), dma((4,)), dma((4,)), dma((4,)), dma((4,)),
-            dma((4,)), dma((4,)),
+            dma((12,)), dma((3,)), dma((8,)), dma((8,)), dma((8,)), dma((8,)), dma((8,)), dma((8,)), dma((8,)),
+            dma((4,)), dma((4,)), pltpu.SemaphoreType.REGULAR((3,)),
         ],
         compiler_params=pltpu.CompilerParams(
             collective_id=0, has_side_effects=True, vmem_limit_bytes=60 * 1024 * 1024
@@ -833,6 +866,31 @@
         table["tx"], table["ix"], table["ty"], table["zf"], table["zi"], table["ti"], table["txc"], table["tyc"],
         table["zfc"], table["zic"], table["tic"], table["ixc"],
     )
+    layer_out, grad_out, gspec = pl.pallas_call(
+        finish,
+        grid=(4,),
+        out_shape=[
+            jax.ShapeDtypeStruct((512, 8, 256), BF16),
+            jax.ShapeDtypeStruct((512, 8, 256), BF16),
+            jax.ShapeDtypeStruct((2, 32, 64, 32), F32),
+        ],
+        in_specs=[
+            pl.BlockSpec((1, 1, PAIRS, 128), lambda i: (i % 2, i // 2, 0, 0)),
+            pl.BlockSpec((1, 1, 8, 128), lambda i: (i % 2, 0, 1, 0)),
+            pl.BlockSpec((2, 8, 128, 128), lambda i: (0, 0, i, 0)),
+            pl.BlockSpec((128, 8, 256), lambda i: (i, 0, 0)),
+            pl.BlockSpec((2, 8, 64, 32), lambda i: (0, i, 0, 0)),
+            pl.BlockSpec((40, 256), lambda i: (0, 0)),
+        ],
+        out_specs=[
+            pl.BlockSpec((128, 8, 256), lambda i: (i, 0, 0)),
+            pl.BlockSpec((128, 8, 256), lambda i: (i, 0, 0)),
+            pl.BlockSpec((2, 8, 64, 32), lambda i: (0, i, 0, 0)),
+        ],
+        scratch_shapes=[f32(PAIRS, 128), f32(2, 1024, 128)],
+        compiler_params=pltpu.CompilerParams(vmem_limit_bytes=60 * 1024 * 1024),
+        name="finish",
+    )(spectrum, spectrum, direct.reshape(2, 8, 512, 128), layer, gspec, table["ix"])
     shape = (32, 16, 8, 256)
     gspec = gspec.reshape(2, 32, 16, 1, 4, 32).transpose(0, 1, 5, 2, 3, 4)
     return layer_out.reshape(shape), grad_out.reshape(shape), gspec

time: 128 us -> 116 us (0.906)
  local copies, waits for them, and re-layouts: 6.95 us -> 0 us
  Pallas kernels: 120 us -> 116 us
    pallas_call x1, Pallas kernels: 120 us -> 108 us  [body(): pl.pallas_call(kernel, out_shape=[jax.ShapeDtypeStruct((512, 8, 256), BF1...]
    pallas_call x0 -> x1, Pallas kernels: none -> 7.32 us  [body(): pl.pallas_call(finish, grid=(4,), out_shape=[jax.ShapeDtypeStruct((512, 8...]
    unnamed x7 -> x0, local copies, waits for them, and re-layouts: 6.95 us -> none
where the time goes in v1:
time: 116 us
  Pallas kernels  116 us (100%)
    pallas_call x1, Pallas kernels, body(): pl.pallas_call(kernel, out_shape=[jax.ShapeDtypeStruct((512, 8, 256), BF1...  108 us
    pallas_call x1, Pallas kernels, body(): pl.pallas_call(finish, grid=(4,), out_shape=[jax.ShapeDtypeStruct((512, 8...  7.32 us

profile of v1, /device:TPU:1, one launch (start us, length us, event | category | flops | bytes accessed | tf_op | source)
XLA Modules:
  0.0 116.3 jit_solution(6787760899389201593)
XLA Ops:
  0.6 108.4 %fno_layer.1 = (bf16[512,8,256]{2,1,0:T(8,128)(2,1)}, f32[2,4096,128]{2,1,0:T(8,128)}, f32[2,32,64,32]{3,2,1,0:T(8,128)}, f32[2,2,320,128]{3,2,1,0:T(8,128)}) custom-call(bf16[512,8,256]{2,1,0:T(8,128)(2,1)} %bitcast.19, bf16[512,8,256]{2,1,0:T(8,128)(2,1)} %bitcast.20, bf16[32,32]{1,0:T(8,128)(2,1)} %w_fine.1, f32[2,32,64,32]{3,2,1,0:T(8,128)} %bitcast.21, ...), custom_call_target="tpu_custom_call" | custom-call | tf_op jit(solution)/shard_map/fno_layer/pallas_call | solution.py:831
  109.0 7.3 %finish.1 = (bf16[512,8,256]{2,1,0:T(8,128)(2,1)}, bf16[512,8,256]{2,1,0:T(8,128)(2,1)}, f32[2,32,64,32]{3,2,1,0:T(8,128)}) custom-call(f32[2,2,320,128]{3,2,1,0:T(8,128)} %get-tuple-element.10.g_ref.zero_ref, f32[2,2,320,128]{3,2,1,0:T(8,128)} %get-tuple-element.10.g_ref.zero_ref, f32[2,8,512,128]{3,2,1,0:T(8,128)} %bitcast.17, ...), custom_call_target="tpu_custom_call" | custom-call | tf_op jit(solution)/shard_map/finish/pallas_call | solution.py:869

commit v2 on v1

--- a/solution.py
+++ b/solution.py
@@ -252,9 +252,10 @@
 
 
 def kernel(
-    feat_hbm, cot_hbm, w_fine, spec_hbm, lift, w_coarse, spec_c_hbm, project,
-    tx_in, ix_in, ty_hbm, zf_hbm, zi_hbm, ti_hbm, txc_in, tyc_in, zfc_hbm, zic_hbm, tic_in, ixc_in,
+    feat_hbm, cot_hbm, w_fine_hbm, spec_hbm, lift_hbm, w_coarse_hbm, spec_c_hbm, project_hbm,
+    tx_hbm, ix_hbm, ty_hbm, zf_hbm, zi_hbm, ti_hbm, txc_hbm, tyc_hbm, zfc_hbm, zic_hbm, tic_hbm, ixc_hbm,
     layer_hbm, dir_hbm, gspec_hbm, g_hbm,
+    w_fine, lift, w_coarse, project, tx_in, ix_in, txc_in, tyc_in, tic_in, ixc_in,
     b0, b1, b2, fy, gph, gpl, feat, cot, spec, spec_c, layer_out, gspec,
     ty, tye, zf, zi, ti, tie, zfc, zic, zfull_h, zfull_l, zifull_h, zifull_l,
     tx, ix, ty_s, tye_s, zf_s, zi_s, ti_s, tie_s,
@@ -274,12 +275,15 @@
     regular = 1 - is0 - is16
 
     loads = [
-        (feat_hbm, feat), (cot_hbm, cot), (spec_hbm, spec), (spec_c_hbm, spec_c),
+        (feat_hbm, feat), (tx_hbm, tx_in), (ix_hbm, ix_in), (txc_hbm, txc_in), (w_fine_hbm, w_fine),
+        (lift_hbm, lift), (w_coarse_hbm, w_coarse), (project_hbm, project), (tyc_hbm, tyc_in),
+        (tic_hbm, tic_in), (ixc_hbm, ixc_in),
+        (cot_hbm, cot), (spec_hbm, spec), (spec_c_hbm, spec_c),
         (ty_hbm.at[kind], ty), (ty_hbm.at[4], tye), (zf_hbm.at[mine], zf), (zi_hbm.at[mine], zi),
         (ti_hbm.at[kind], ti), (ti_hbm.at[4], tie), (zfc_hbm.at[mine], zfc), (zic_hbm.at[mine], zic),
     ]
     loads = [pltpu.make_async_copy(a, b, load_sem.at[n]) for n, (a, b) in enumerate(loads)]
-    for load in loads:
+    for load in loads[:4]:
         load.start()
 
     barrier = pltpu.get_barrier_semaphore()
@@ -296,6 +300,8 @@
         tell(barrier, me, lax.rem(mine + 2 * t, NPY))
     other = 2 * lax.div(mine, 2) + 1 - lax.rem(mine, 2)
     tell(barrier, me, other)
+    for load in loads[4:]:
+        load.start()
     pl.semaphore_wait(barrier, 14)
     for t in range(1, 4):
         tell(here.at[0], lax.rem(me + 8 * t, NPX), mine)
@@ -304,22 +310,43 @@
         h = lax.div(d + 15, 32)
         return h, pl.multiple_of(16 * (d * (1 - 2 * h) + 32 * h), 16)
 
+    pending = []
+
+    def left(semaphore, ref, condition=None):
+        def wait():
+            pltpu.make_async_copy(ref, ref, semaphore).wait()
+
+        pending.append(wait if condition is None else lambda: pl.when(condition)(wait))
+
+    slab, side = lax.div(mine, 2), lax.rem(mine, 2)
+
+    def each_px(send):
+        def step(t, carry):
+            send(lax.rem(me + t, NPX))
+            return carry
+
+        lax.fori_loop(1, NPX, step, 0)
+
+    def each_py(send):
+        for far, ahead in ((1, 2), (1, 1), (1, 3), (1, 0), (0, 2), (0, 1), (0, 3)):
+            send(2 * lax.rem(slab + ahead, 4) + (1 - side if far else side))
+
     def at16(d):
         return pl.ds(pl.multiple_of(16 * d, 16), 16)
 
     def px_forward(n, t):
         k = 4 * n + t
-
-        def send(step, carry):
-            d = lax.rem(me + step, NPX)
+        left(px_send.at[k], rx.at[0, 0, pl.ds(0, 496)])
+        left(pxe_send.at[k], rx.at[0, 0, pl.ds(0, 16)], is16 == 0)
+
+        def send(d):
             h, row = pair_row(d)
             pltpu.make_async_remote_copy(
                 s_buf.at[n, t, h, pl.ds(row, 16)], rx.at[n, t, at16(me)],
                 px_send.at[k], px_recv.at[k], device_id={"px": d, "py": mine}, device_id_type=MESH,
             ).start()
-            return carry
-
-        lax.fori_loop(1, NPX, send, 0)
+
+        each_px(send)
         h, row = pair_row(me)
         pltpu.make_async_copy(s_buf.at[n, t, h, pl.ds(row, 16)], rx.at[n, t, at16(me)], px_recv.at[k]).start()
 
@@ -346,30 +373,28 @@
 
     def px_inverse(n, t, target):
         k = 4 * n + 2 + t
+        left(px_send.at[k], rx.at[0, 0, pl.ds(0, 496)])
+        left(pxe_send.at[k], rx.at[0, 0, pl.ds(0, 496)], is16 == 1)
         h, row = pair_row(me)
 
-        def send(step, carry):
-            d = lax.rem(me + step, NPX)
+        def send(d):
             pltpu.make_async_remote_copy(
                 sv.at[n, t, at16(d)], target.at[t, h, pl.ds(row, 16)],
                 px_send.at[k], px_recv.at[k], device_id={"px": d, "py": mine}, device_id_type=MESH,
             ).start()
-            return carry
-
-        lax.fori_loop(1, NPX, send, 0)
+
+        each_px(send)
         pltpu.make_async_copy(sv.at[n, t, at16(me)], target.at[t, h, pl.ds(row, 16)], px_recv.at[k]).start()
 
         @pl.when(is16 == 1)
         def _():
-            def send_extra(step, carry):
-                d = lax.rem(me + step, NPX)
+            def send_extra(d):
                 pltpu.make_async_remote_copy(
                     sve.at[n, t, at16(d)], target.at[t, 1, pl.ds(256, 16)],
                     pxe_send.at[k], pxe_recv.at[k], device_id={"px": d, "py": mine}, device_id_type=MESH,
                 ).start()
-                return carry
-
-            lax.fori_loop(1, NPX, send_extra, 0)
+
+            each_px(send_extra)
             pltpu.make_async_copy(sve.at[n, t, at16(me)], target.at[t, 1, pl.ds(256, 16)], pxe_recv.at[k]).start()
 
     def px_inverse_wait(n, t):
@@ -379,16 +404,17 @@
         pltpu.make_async_copy(some, some, pxe_recv.at[k]).wait()
 
     def py_exchange(slot, source, target):
-        def send(step, carry):
-            p = lax.rem(mine + step, NPY)
-            for q, to in ((0, me), (1, partner)):
+        left(py_send.at[slot], ex.at[0, 0, pl.ds(0, 14)])
+        left(pye_send.at[slot], ex.at[0, 0, 0], regular == 1)
+
+        def send(p):
+            for q, to in ((1, partner), (0, me)):
                 pltpu.make_async_remote_copy(
                     source(q, p), target.at[8 * q + mine], py_send.at[slot], py_recv.at[slot],
                     device_id={"px": to, "py": p}, device_id_type=MESH,
                 ).start()
-            return carry
-
-        lax.fori_loop(1, NPY, send, 0)
+
+        each_py(send)
         pltpu.make_async_copy(source(0, mine), target.at[mine], py_recv.at[slot]).start()
 
         @pl.when(regular == 1)
@@ -406,29 +432,28 @@
         pltpu.make_async_copy(target, target, py_recv.at[slot]).wait()
 
     def coarse_px(slot, source, target):
+        left(c_send.at[slot], target.at[pl.ds(0, 248)])
         there = target.at[pl.ds(pl.multiple_of(8 * me, 8), 8)]
 
-        def send(t, carry):
-            d = lax.rem(me + t, NPX)
+        def send(d):
             pltpu.make_async_remote_copy(
                 source.at[pl.ds(pl.multiple_of(8 * d, 8), 8)], there, c_send.at[slot], c_recv.at[slot],
                 device_id={"px": d, "py": mine}, device_id_type=MESH,
             ).start()
-            return carry
-
-        lax.fori_loop(1, NPX, send, 0)
+
+        each_px(send)
         pltpu.make_async_copy(source.at[pl.ds(pl.multiple_of(8 * me, 8), 8)], there, c_recv.at[slot]).start()
 
     def coarse_py(slot, source, target):
-        def send(t, carry):
-            p = lax.rem(mine + t, NPY)
+        left(c_send.at[slot], target.at[pl.ds(0, 7)])
+
+        def send(p):
             pltpu.make_async_remote_copy(
                 source(p), target.at[mine], c_send.at[slot], c_recv.at[slot],
                 device_id={"px": me, "py": p}, device_id_type=MESH,
             ).start()
-            return carry
-
-        lax.fori_loop(1, NPY, send, 0)
+
+        each_py(send)
         pltpu.make_async_copy(source(mine), target.at[mine], c_recv.at[slot]).start()
 
     def coarse_wait(slot, target):
@@ -551,11 +576,12 @@
         for h in range(2):
             s_buf[n, t, h, pl.ds(y, 40, stride=8), :] = both[:, 128 * h : 128 * h + 128]
 
+    for n in range(4):
+        loads[n].wait()
     high, low = split(tx_in[...])
     tx[pl.ds(0, 40), :] = high
     tx[pl.ds(40, 40), :] = low
     ix[...] = stacked_table(ix_in[...])
-    loads[0].wait()
     for t in range(2):
         unpack(b0, feat, t)
 
@@ -576,6 +602,9 @@
     g_buf[:, :, pl.ds(272, 48), :] = jnp.zeros((2, 2, 48, 128), F32)
     g_buf[:, 1, pl.ds(0, 16), :] = jnp.zeros((2, 16, 128), F32)
     sc[...] = jnp.zeros((256, 128), F32)
+
+    for n in range(4, 11):
+        loads[n].wait()
 
     txc_high, txc_low = split(txc_in[...])
     pool = ones_where(iota((128, 512), 0) == (iota((128, 512), 1) >> 2))
@@ -588,8 +617,6 @@
         high, low = split(total)
         part = dot3(txc_high, txc_low, high, low, ((1,), (1,)))
         sc[pl.ds(big, 64, stride=4), :] = part
-    coarse_px(0, sc, rc)
-
     pl.semaphore_wait(here.at[1], 3)
     tell(here.at[2], me, other)
 
@@ -601,7 +628,7 @@
         return carry
 
     lax.fori_loop(0, 8, local, 0)
-    loads[1].wait()
+    loads[11].wait()
     for t in range(2):
         unpack(b1, cot, t)
     low_total = jnp.zeros((128, 128), F32)
@@ -610,7 +637,7 @@
         high, low = split(rst[big])
         low_total = low_total + dot(high, gather) + dot(low, gather)
     rst2[...] = low_total
-    for n in range(2, 12):
+    for n in range(12, 22):
         loads[n].wait()
     for whole, parts in ((ty, ty_s), (tye, tye_s), (zf, zf_s), (zi, zi_s), (ti, ti_s), (tie, tie_s)):
         high, low = split(whole[...])
@@ -639,6 +666,15 @@
         px_forward_wait(0, t)
         forward_yz(0, t)
 
+    coarse_px(0, sc, rc)
+
+    real, imag = gather_modes(0)
+    modes[0] = real
+    modes[1] = imag
+    out_real, out_imag = mix_modes(spec, real, imag, 32)
+    fine_factor = mode_factor(256.0 * 256.0 * 128.0)
+    spread_modes(0, out_real * fine_factor, out_imag * fine_factor)
+
     coarse_wait(0, rc)
     high, low = split(rc[...])
     along_y = dot3(*split(tyc_in[...]), high, low)
@@ -648,33 +684,8 @@
     exc[...] = jnp.where(dup, full[:, :512], full[:, 512:]).reshape(8, 8, 512)
     coarse_py(1, lambda p: exc.at[p], rec)
 
-    real, imag = gather_modes(0)
-    modes[0] = real
-    modes[1] = imag
-    out_real, out_imag = mix_modes(spec, real, imag, 32)
-    fine_factor = mode_factor(256.0 * 256.0 * 128.0)
-    spread_modes(0, out_real * fine_factor, out_imag * fine_factor)
-
-    coarse_wait(1, rec)
-    real, imag = to_modes(jnp.sum(rec[...], axis=0), 32)
-    high, low = split(jnp.concatenate([real, imag], axis=0))
-    lifted = dot(high, lift[...]) + dot(low, lift[...])
-    out_real, out_imag = mix_modes(spec_c, lifted[:64], lifted[64:], 64)
-    coarse_factor = mode_factor(64.0 * 64.0 * 32.0)
-    hc[...] = from_modes(out_real * coarse_factor, out_imag * coarse_factor, 64)
-    coarse_py(2, lambda p: hc, ric)
-
     for t in range(2):
         inverse_zy(0, t, g_buf)
-
-    coarse_wait(2, ric)
-    high, low = split(ric[...].reshape(64, 1024))
-    along_z = dot3(high, low, zifull_h[...], zifull_l[...])
-    high, low = split(jnp.concatenate([along_z[:, :256], along_z[:, 256:]], axis=0))
-    along_y = dot3(*split(tic_in[...]), high, low)
-    for hh in range(2):
-        svc[pl.ds(hh, 128, stride=2), :] = along_y[:, 128 * hh : 128 * hh + 128]
-    coarse_px(3, svc, gc)
 
     for t in range(2):
         px_inverse_wait(0, t)
@@ -707,6 +718,48 @@
     writes = [pltpu.make_async_copy(b1, dir_hbm, out_sem.at[0])]
     writes[0].start()
 
+    coarse_wait(1, rec)
+    real, imag = to_modes(jnp.sum(rec[...], axis=0), 32)
+    high, low = split(jnp.concatenate([real, imag], axis=0))
+    lifted = dot(high, lift[...]) + dot(low, lift[...])
+    out_real, out_imag = mix_modes(spec_c, lifted[:64], lifted[64:], 64)
+    coarse_factor = mode_factor(64.0 * 64.0 * 32.0)
+    hc[...] = from_modes(out_real * coarse_factor, out_imag * coarse_factor, 64)
+    for t in range(2):
+        px_forward_wait(1, t)
+        forward_yz(1, t)
+    coarse_py(2, lambda p: hc, ric)
+
+    real, imag = gather_modes(1)
+    real, imag = real * fine_factor, imag * fine_factor
+    lane = iota((64, 32), 1)
+    pull_real = jnp.zeros((64, 32), F32)
+    pull_imag = jnp.zeros((64, 32), F32)
+    for i in range(32):
+        w0, w1 = spec[0, i], spec[1, i]
+        a = jnp.sum(w0 * real + w1 * imag, axis=1, keepdims=True)
+        b = jnp.sum(w0 * imag - w1 * real, axis=1, keepdims=True)
+        pull_real = jnp.where(lane == i, a, pull_real)
+        pull_imag = jnp.where(lane == i, b, pull_imag)
+    spread_modes(1, pull_real, pull_imag)
+    coarse_wait(2, ric)
+    high, low = split(ric[...].reshape(64, 1024))
+    along_z = dot3(high, low, zifull_h[...], zifull_l[...])
+    high, low = split(jnp.concatenate([along_z[:, :256], along_z[:, 256:]], axis=0))
+    along_y = dot3(*split(tic_in[...]), high, low)
+    for hh in range(2):
+        svc[pl.ds(hh, 128, stride=2), :] = along_y[:, 128 * hh : 128 * hh + 128]
+    coarse_px(3, svc, gc)
+
+    x_real, x_imag = modes[0], modes[1]
+    for i in range(32):
+        a, b = column(x_real, i), column(x_imag, i)
+        gspec[0, i] = real * a + imag * b
+        gspec[1, i] = imag * a - real * b
+    writes.append(pltpu.make_async_copy(gspec, gspec_hbm, out_sem.at[2]))
+    writes[1].start()
+    for t in range(2):
+        inverse_zy(1, t, g_hbm)
     coarse_wait(3, gc)
     halves_out = []
     for hh in range(2):
@@ -733,63 +786,15 @@
             put(b2, y, block(b0, y) + prolonged)
     pack(layer_out, b2)
     writes.append(pltpu.make_async_copy(layer_out, layer_hbm, out_sem.at[1]))
-    writes[1].start()
-
-    for t in range(2):
-        px_forward_wait(1, t)
-        forward_yz(1, t)
-    real, imag = gather_modes(1)
-    real, imag = real * fine_factor, imag * fine_factor
-    lane = iota((64, 32), 1)
-    pull_real = jnp.zeros((64, 32), F32)
-    pull_imag = jnp.zeros((64, 32), F32)
-    for i in range(32):
-        w0, w1 = spec[0, i], spec[1, i]
-        a = jnp.sum(w0 * real + w1 * imag, axis=1, keepdims=True)
-        b = jnp.sum(w0 * imag - w1 * real, axis=1, keepdims=True)
-        pull_real = jnp.where(lane == i, a, pull_real)
-        pull_imag = jnp.where(lane == i, b, pull_imag)
-    spread_modes(1, pull_real, pull_imag)
-    x_real, x_imag = modes[0], modes[1]
-    for i in range(32):
-        a, b = column(x_real, i), column(x_imag, i)
-        gspec[0, i] = real * a + imag * b
-        gspec[1, i] = imag * a - real * b
-    writes.append(pltpu.make_async_copy(gspec, gspec_hbm, out_sem.at[2]))
     writes[2].start()
-    for t in range(2):
-        inverse_zy(1, t, g_hbm)
+
     for t in range(2):
         px_inverse_wait(1, t)
 
     for write in writes:
         write.wait()
-    for k in range(8):
-        most = rx.at[0, 0, pl.ds(0, 496)]
-        pltpu.make_async_copy(most, most, px_send.at[k]).wait()
-        if k % 4 < 2:
-
-            @pl.when(is16 == 0)
-            def _():
-                some = rx.at[0, 0, pl.ds(0, 16)]
-                pltpu.make_async_copy(some, some, pxe_send.at[k]).wait()
-
-        else:
-
-            @pl.when(is16 == 1)
-            def _():
-                pltpu.make_async_copy(most, most, pxe_send.at[k]).wait()
-
-    for slot in range(8):
-        some = ex.at[0, 0, pl.ds(0, 14)]
-        pltpu.make_async_copy(some, some, py_send.at[slot]).wait()
-
-        @pl.when(regular == 1)
-        def _():
-            pltpu.make_async_copy(ex.at[0, 0, 0], ex.at[0, 0, 0], pye_send.at[slot]).wait()
-
-    for slot, most in ((0, rc.at[pl.ds(0, 248)]), (1, exc.at[pl.ds(0, 7)]), (2, ric.at[pl.ds(0, 7)]), (3, gc.at[pl.ds(0, 248)])):
-        pltpu.make_async_copy(most, most, c_send.at[slot]).wait()
+    for wait in pending:
+        wait()
 
 
 def finish(g_ref, zero_ref, dir_ref, layer_ref, gspec_ref, ix_in, layer_out, grad_out, gspec_out, kept, mixed):
@@ -818,7 +823,6 @@
     table = tables()
     fine = spectral_fine.transpose(0, 1, 3, 4, 5, 2).reshape(2, 32, 64, 32)
     coarse = spectral_coarse.transpose(0, 1, 3, 4, 5, 2).reshape(2, 64, 64, 64)
-    vmem = pl.BlockSpec(memory_space=pltpu.VMEM)
     hbm = pl.BlockSpec(memory_space=pl.ANY)
 
     def f32(*shape):
@@ -836,9 +840,11 @@
             jax.ShapeDtypeStruct((2, 32, 64, 32), F32),
             jax.ShapeDtypeStruct((2, 2, PAIRS, 128), F32),
         ],
-        in_specs=[hbm, hbm, vmem, hbm, vmem, vmem, hbm, vmem, vmem, vmem, hbm, hbm, hbm, hbm, vmem, vmem, hbm, hbm, vmem, vmem],
+        in_specs=[hbm] * 20,
         out_specs=[hbm] * 4,
         scratch_shapes=[
+            bf16(32, 32), bf16(32, 64), bf16(64, 64), bf16(32, 64), f32(40, 256), f32(40, 256), f32(64, 256),
+            f32(128, 256), f32(128, 128), f32(128, 128),
             f32(2, 4096, 128), f32(2, 4096, 128), f32(2, 4096, 128),
             bf16(8, 512, 256), bf16(8, 512, 256), bf16(8, 512, 256),
             bf16(512, 8, 256), bf16(512, 8, 256), f32(2, 32, 64, 32), f32(2, 64, 64, 64),
@@ -853,7 +859,7 @@
             f32(2, 2, 2, 8, 128), f32(2, 2, 16, 8, 128), f32(2, 2, 512, 128), f32(2, 2, 512, 128), f32(2, 2, PAIRS, 128),
             f32(256, 128), f32(256, 128), f32(8, 8, 512), f32(8, 8, 512), f32(8, 1024), f32(8, 8, 1024),
             f32(256, 128), f32(256, 128),
-            dma((12,)), dma((3,)), dma((8,)), dma((8,)), dma((8,)), dma((8,)), dma((8,)), dma((8,)), dma((8,)),
+            dma((22,)), dma((3,)), dma((8,)), dma((8,)), dma((8,)), dma((8,)), dma((8,)), dma((8,)), dma((8,)),
             dma((4,)), dma((4,)), pltpu.SemaphoreType.REGULAR((3,)),
         ],
         compiler_params=pltpu.CompilerParams(

time: 116 us -> 110 us (0.948)
  Pallas kernels: 116 us -> 109 us
    pallas_call x1, Pallas kernels: 108 us -> 102 us  [body(): pl.pallas_call(kernel, out_shape=[jax.ShapeDtypeStruct((512, 8, 256), BF1...]
where the time goes in v2:
time: 110 us; the launch traced here: 109 us
  Pallas kernels  109 us (99%)
    pallas_call x1, Pallas kernels, body(): pl.pallas_call(kernel, out_shape=[jax.ShapeDtypeStruct((512, 8, 256), BF1...  102 us
    pallas_call x1, Pallas kernels, body(): pl.pallas_call(finish, grid=(4,), out_shape=[jax.ShapeDtypeStruct((512, 8...  7.31 us

profile of v2, /device:TPU:1, one launch (start us, length us, event | category | flops | bytes accessed | tf_op | source)
XLA Modules:
  0.0 109.5 jit_solution(13547254126561756922)
XLA Ops:
  0.6 101.5 %fno_layer.1 = (bf16[512,8,256]{2,1,0:T(8,128)(2,1)}, f32[2,4096,128]{2,1,0:T(8,128)}, f32[2,32,64,32]{3,2,1,0:T(8,128)}, f32[2,2,320,128]{3,2,1,0:T(8,128)}) custom-call(bf16[512,8,256]{2,1,0:T(8,128)(2,1)} %bitcast.19, bf16[512,8,256]{2,1,0:T(8,128)(2,1)} %bitcast.20, bf16[32,32]{1,0:T(8,128)(2,1)} %w_fine_hbm.1, f32[2,32,64,32]{3,2,1,0:T(8,128)} %bitcast.21, ...), custom_call_target="tpu_custom_call" | custom-call | tf_op jit(solution)/shard_map/fno_layer/pallas_call | solution.py:835
  102.2 7.3 %finish.1 = (bf16[512,8,256]{2,1,0:T(8,128)(2,1)}, bf16[512,8,256]{2,1,0:T(8,128)(2,1)}, f32[2,32,64,32]{3,2,1,0:T(8,128)}) custom-call(f32[2,2,320,128]{3,2,1,0:T(8,128)} %get-tuple-element.10.g_ref.zero_ref, f32[2,2,320,128]{3,2,1,0:T(8,128)} %get-tuple-element.10.g_ref.zero_ref, f32[2,8,512,128]{3,2,1,0:T(8,128)} %bitcast.17, ...), custom_call_target="tpu_custom_call" | custom-call | tf_op jit(solution)/shard_map/finish/pallas_call | solution.py:875

commit v3 on v2

--- a/solution.py
+++ b/solution.py
@@ -260,7 +260,7 @@
     ty, tye, zf, zi, ti, tie, zfc, zic, zfull_h, zfull_l, zifull_h, zifull_l,
     tx, ix, ty_s, tye_s, zf_s, zi_s, ti_s, tie_s,
     wk, wkt, yc, rst, rst2, modes,
-    s_buf, rx, rxe, ex, re_buf, hq, ri, sv, sve, g_buf,
+    s_buf, rx, rxe, ex, re_buf, hq, ri, sv, g_buf,
     sc, rc, exc, rec, hc, ric, svc, gc,
     load_sem, out_sem, px_send, px_recv, pxe_send, pxe_recv, py_send, py_recv, pye_send,
     c_send, c_recv, here,
@@ -373,35 +373,39 @@
 
     def px_inverse(n, t, target):
         k = 4 * n + 2 + t
-        left(px_send.at[k], rx.at[0, 0, pl.ds(0, 496)])
-        left(pxe_send.at[k], rx.at[0, 0, pl.ds(0, 496)], is16 == 1)
+        left(px_send.at[k], rx.at[0, 0, pl.ds(0, 496)], is16 == 0)
+        left(px_send.at[k], rx.at[0, :, pl.ds(0, 496)], is16 == 1)
         h, row = pair_row(me)
 
-        def send(d):
-            pltpu.make_async_remote_copy(
-                sv.at[n, t, at16(d)], target.at[t, h, pl.ds(row, 16)],
-                px_send.at[k], px_recv.at[k], device_id={"px": d, "py": mine}, device_id_type=MESH,
+        @pl.when(is16 == 0)
+        def _():
+            def send(d):
+                pltpu.make_async_remote_copy(
+                    sv.at[n, t, 0, at16(d)], target.at[t, h, pl.ds(row, 16)],
+                    px_send.at[k], px_recv.at[k], device_id={"px": d, "py": mine}, device_id_type=MESH,
+                ).start()
+
+            each_px(send)
+            pltpu.make_async_copy(
+                sv.at[n, t, 0, at16(me)], target.at[t, h, pl.ds(row, 16)], px_recv.at[k]
             ).start()
-
-        each_px(send)
-        pltpu.make_async_copy(sv.at[n, t, at16(me)], target.at[t, h, pl.ds(row, 16)], px_recv.at[k]).start()
 
         @pl.when(is16 == 1)
         def _():
-            def send_extra(d):
+            def send(d):
                 pltpu.make_async_remote_copy(
-                    sve.at[n, t, at16(d)], target.at[t, 1, pl.ds(256, 16)],
-                    pxe_send.at[k], pxe_recv.at[k], device_id={"px": d, "py": mine}, device_id_type=MESH,
+                    sv.at[n, t, :, at16(d)], target.at[t, :, pl.ds(256, 16)],
+                    px_send.at[k], px_recv.at[k], device_id={"px": d, "py": mine}, device_id_type=MESH,
                 ).start()
 
-            each_px(send_extra)
-            pltpu.make_async_copy(sve.at[n, t, at16(me)], target.at[t, 1, pl.ds(256, 16)], pxe_recv.at[k]).start()
+            each_px(send)
+            pltpu.make_async_copy(
+                sv.at[n, t, :, at16(me)], target.at[t, :, pl.ds(256, 16)], px_recv.at[k]
+            ).start()
 
     def px_inverse_wait(n, t):
-        k = 4 * n + 2 + t
-        pltpu.make_async_copy(rx.at[n, t], rx.at[n, t], px_recv.at[k]).wait()
-        some = rx.at[n, t, pl.ds(0, 16)]
-        pltpu.make_async_copy(some, some, pxe_recv.at[k]).wait()
+        some = rx.at[n, :, pl.ds(0, 264)]
+        pltpu.make_async_copy(some, some, px_recv.at[4 * n + 2 + t]).wait()
 
     def py_exchange(slot, source, target):
         left(py_send.at[slot], ex.at[0, 0, pl.ds(0, 14)])
@@ -506,11 +510,11 @@
         high, low = split(ri[n, t].reshape(128, 128))
         full = dot3(high, low, zi_s[0], zi_s[1])
         high, low = split(jnp.concatenate([full[:, :128], full[:, 128:]], axis=0))
-        sv[n, t] = dot3(ti_s[0], ti_s[1], high, low)
+        sv[n, t, 0] = dot3(ti_s[0], ti_s[1], high, low)
 
         @pl.when(is16 == 1)
         def _():
-            sve[n, t] = dot3(tie_s[0], tie_s[1], high, low)
+            sv[n, t, 1] = dot3(tie_s[0], tie_s[1], high, low)
 
         px_inverse(n, t, target)
 
@@ -592,7 +596,7 @@
             store_pairs(0, t, y, both[:40] + both[40:])
             return carry
 
-        lax.fori_loop(0, 8, analyse_x, 0)
+        lax.fori_loop(0, 8, analyse_x, 0, unroll=2)
         fix_zero(0, t)
         if t == 0:
             pl.semaphore_wait(here.at[0], 3)
@@ -695,10 +699,10 @@
             value = jnp.concatenate([g_buf[t, h, pl.ds(y, 40, stride=8), :] for h in range(2)], axis=1)
             pre = some_rows(b2, t, y) + synthesise_x(value, ix[...])
             square = pre * pre
-            tanh = jnp.tanh(ROOT * pre * (1.0 + 0.044715 * square))
-            half = 0.5 * (1.0 + tanh)
-            put_part(b0, t, y, pre * half)
-            slope = half + 0.5 * pre * (1.0 - tanh * tanh) * (ROOT + (3.0 * 0.044715 * ROOT) * square)
+            half = 0.5 + 0.5 * jnp.tanh(pre * (ROOT + (0.044715 * ROOT) * square))
+            act = pre * half
+            put_part(b0, t, y, act)
+            slope = half + act * (1.0 - half) * (2.0 * ROOT + (6.0 * 0.044715 * ROOT) * square)
             high, low = split(take(b1, t, y) * slope)
             put_rows(gph, t, y, high)
             put_rows(gpl, t, y, low)
@@ -706,7 +710,7 @@
             store_pairs(1, t, y, both[:40] + both[40:] + dot(tx[pl.ds(0, 40), :], low, ((1,), (1,))))
             return carry
 
-        lax.fori_loop(0, 8, middle, 0)
+        lax.fori_loop(0, 8, middle, 0, unroll=2)
         fix_zero(1, t)
         px_forward(1, t)
 
@@ -856,7 +860,7 @@
             bf16(2, 512, 256), bf16(2, 512, 256),
             bf16(512, 512), bf16(512, 512), f32(256, 128), f32(2, 128, 256), f32(128, 128), f32(2, 64, 32),
             f32(2, 2, 2, PAIRS, 128), f32(2, 2, 512, 128), f32(2, 2, 512, 128), f32(2, 2, 16, 8, 128), f32(2, 2, 16, 8, 128),
-            f32(2, 2, 2, 8, 128), f32(2, 2, 16, 8, 128), f32(2, 2, 512, 128), f32(2, 2, 512, 128), f32(2, 2, PAIRS, 128),
+            f32(2, 2, 2, 8, 128), f32(2, 2, 16, 8, 128), f32(2, 2, 2, 512, 128), f32(2, 2, PAIRS, 128),
             f32(256, 128), f32(256, 128), f32(8, 8, 512), f32(8, 8, 512), f32(8, 1024), f32(8, 8, 1024),
             f32(256, 128), f32(256, 128),
             dma((22,)), dma((3,)), dma((8,)), dma((8,)), dma((8,)), dma((8,)), dma((8,)), dma((8,)), dma((8,)),

time: 110 us -> 110 us (level)
  no operation moved by 1% of the time
where the time goes in v3:
time: 110 us
  Pallas kernels  109 us (99%)
    pallas_call x1, Pallas kernels, body(): pl.pallas_call(kernel, out_shape=[jax.ShapeDtypeStruct((512, 8, 256), BF1...  102 us
    pallas_call x1, Pallas kernels, body(): pl.pallas_call(finish, grid=(4,), out_shape=[jax.ShapeDtypeStruct((512, 8...  7.32 us

profile of v3, /device:TPU:1, one launch (start us, length us, event | category | flops | bytes accessed | tf_op | source)
XLA Modules:
  0.0 109.7 jit_solution(14479388567125470165)
XLA Ops:
  0.6 101.7 %fno_layer.1 = (bf16[512,8,256]{2,1,0:T(8,128)(2,1)}, f32[2,4096,128]{2,1,0:T(8,128)}, f32[2,32,64,32]{3,2,1,0:T(8,128)}, f32[2,2,320,128]{3,2,1,0:T(8,128)}) custom-call(bf16[512,8,256]{2,1,0:T(8,128)(2,1)} %bitcast.19, bf16[512,8,256]{2,1,0:T(8,128)(2,1)} %bitcast.20, bf16[32,32]{1,0:T(8,128)(2,1)} %w_fine_hbm.1, f32[2,32,64,32]{3,2,1,0:T(8,128)} %bitcast.21, ...), custom_call_target="tpu_custom_call" | custom-call | tf_op jit(solution)/shard_map/fno_layer/pallas_call | solution.py:839
  102.4 7.3 %finish.1 = (bf16[512,8,256]{2,1,0:T(8,128)(2,1)}, bf16[512,8,256]{2,1,0:T(8,128)(2,1)}, f32[2,32,64,32]{3,2,1,0:T(8,128)}) custom-call(f32[2,2,320,128]{3,2,1,0:T(8,128)} %get-tuple-element.10.g_ref.zero_ref, f32[2,2,320,128]{3,2,1,0:T(8,128)} %get-tuple-element.10.g_ref.zero_ref, f32[2,8,512,128]{3,2,1,0:T(8,128)} %bitcast.17, ...), custom_call_target="tpu_custom_call" | custom-call | tf_op jit(solution)/shard_map/finish/pallas_call | solution.py:879

commit v4 on v3

--- a/solution.py
+++ b/solution.py
@@ -758,8 +758,9 @@
     x_real, x_imag = modes[0], modes[1]
     for i in range(32):
         a, b = column(x_real, i), column(x_imag, i)
-        gspec[0, i] = real * a + imag * b
-        gspec[1, i] = imag * a - real * b
+        lanes = pl.ds(32 * (i % 4), 32)
+        gspec[0, i // 4, :, lanes] = real * a + imag * b
+        gspec[1, i // 4, :, lanes] = imag * a - real * b
     writes.append(pltpu.make_async_copy(gspec, gspec_hbm, out_sem.at[2]))
     writes[1].start()
     for t in range(2):
@@ -817,7 +818,8 @@
     for lane in range(2):
         grad_out[:, :, pl.ds(128 * lane, 128)] = mixed[lane].reshape(128, 8, 128).astype(BF16)
     layer_out[...] = layer_ref[...]
-    gspec_out[...] = gspec_ref[...]
+    for c in range(8):
+        gspec_out[:, c] = gspec_ref[:, c // 4, :, 32 * (c % 4) : 32 * (c % 4) + 32]
 
 
 def body(
@@ -841,7 +843,7 @@
         out_shape=[
             jax.ShapeDtypeStruct((512, 8, 256), BF16),
             jax.ShapeDtypeStruct((2, 4096, 128), F32),
-            jax.ShapeDtypeStruct((2, 32, 64, 32), F32),
+            jax.ShapeDtypeStruct((2, 8, 64, 128), F32),
             jax.ShapeDtypeStruct((2, 2, PAIRS, 128), F32),
         ],
         in_specs=[hbm] * 20,
@@ -852,7 +854,7 @@
             f32(2, 4096, 128), f32(2, 4096, 128), f32(2, 4096, 128),
             bf16(8, 512, 256), bf16(8, 512, 256), bf16(8, 512, 256),
             bf16(512, 8, 256), bf16(512, 8, 256), f32(2, 32, 64, 32), f32(2, 64, 64, 64),
-            bf16(512, 8, 256), f32(2, 32, 64, 32),
+            bf16(512, 8, 256), f32(2, 8, 64, 128),
             f32(256, 512), f32(256, 512), f32(256, 256), f32(128, 256),
             f32(512, 256), f32(512, 256), f32(2, 8, 1024), f32(16, 512),
             bf16(256, 1024), bf16(256, 1024), bf16(1024, 512), bf16(1024, 512),
@@ -889,7 +891,7 @@
             pl.BlockSpec((1, 1, 8, 128), lambda i: (i % 2, 0, 1, 0)),
             pl.BlockSpec((2, 8, 128, 128), lambda i: (0, 0, i, 0)),
             pl.BlockSpec((128, 8, 256), lambda i: (i, 0, 0)),
-            pl.BlockSpec((2, 8, 64, 32), lambda i: (0, i, 0, 0)),
+            pl.BlockSpec((2, 2, 64, 128), lambda i: (0, i, 0, 0)),
             pl.BlockSpec((40, 256), lambda i: (0, 0)),
         ],
         out_specs=[

time: 110 us -> 110 us (level)
  no operation moved by 1% of the time
where the time goes in v4:
time: 110 us; the launch traced here: 109 us
  Pallas kernels  109 us (99%)
    pallas_call x1, Pallas kernels, body(): pl.pallas_call(kernel, out_shape=[jax.ShapeDtypeStruct((512, 8, 256), BF1...  102 us
    pallas_call x1, Pallas kernels, body(): pl.pallas_call(finish, grid=(4,), out_shape=[jax.ShapeDtypeStruct((512, 8...  6.94 us

profile of v4, /device:TPU:1, one launch (start us, length us, event | category | flops | bytes accessed | tf_op | source)
XLA Modules:
  0.0 109.3 jit_solution(3576044592589873639)
XLA Ops:
  0.6 101.7 %fno_layer.1 = (bf16[512,8,256]{2,1,0:T(8,128)(2,1)}, f32[2,4096,128]{2,1,0:T(8,128)}, f32[2,8,64,128]{3,2,1,0:T(8,128)}, f32[2,2,320,128]{3,2,1,0:T(8,128)}) custom-call(bf16[512,8,256]{2,1,0:T(8,128)(2,1)} %bitcast.19, bf16[512,8,256]{2,1,0:T(8,128)(2,1)} %bitcast.20, bf16[32,32]{1,0:T(8,128)(2,1)} %w_fine_hbm.1, f32[2,32,64,32]{3,2,1,0:T(8,128)} %bitcast.21, ...), custom_call_target="tpu_custom_call" | custom-call | tf_op jit(solution)/shard_map/fno_layer/pallas_call | solution.py:841
  102.4 6.9 %finish.1 = (bf16[512,8,256]{2,1,0:T(8,128)(2,1)}, bf16[512,8,256]{2,1,0:T(8,128)(2,1)}, f32[2,32,64,32]{3,2,1,0:T(8,128)}) custom-call(f32[2,2,320,128]{3,2,1,0:T(8,128)} %get-tuple-element.10.g_ref.zero_ref, f32[2,2,320,128]{3,2,1,0:T(8,128)} %get-tuple-element.10.g_ref.zero_ref, f32[2,8,512,128]{3,2,1,0:T(8,128)} %bitcast.17, ...), custom_call_target="tpu_custom_call" | custom-call | tf_op jit(solution)/shard_map/finish/pallas_call | solution.py:881
